TPU v7x, 128 devices: a whole 4x4x4 slice. The times are simulated.
128 devices in a mesh: doc: 4 (over y), resp: 8 (over z, x_hi), prob: 4 (over x_lo, core).
Axes of the slice: x: 4 (x_hi: 2, x_lo: 2; x = x_hi * 2 + x_lo), y: 4, z: 4, core: 2. Of those that a mesh axis runs over, the one named last changes fastest.
Arguments:
- x_doc: bfloat16 [512, 5120], P('doc'), may hold values from -6 to 6
- x_prompt: bfloat16 [4, 1024, 5120], P('prob', 'resp'), may hold values from -6 to 6
- w_key: bfloat16 [5120, 512], replicated, may hold values from -0.078125 to 0.078125
- w_value: bfloat16 [5120, 512], replicated, may hold values from -0.078125 to 0.078125
- queries: bfloat16 [128, 128, 4096], P(('doc', 'resp', 'prob')), may hold values from -240 to 240
- resp_keys: bfloat16 [128, 128, 512], P(('doc', 'resp', 'prob')), may hold values from -6 to 6
- resp_values: bfloat16 [128, 128, 512], P(('doc', 'resp', 'prob')), may hold values from -6 to 6
- out_grad: bfloat16 [128, 128, 4096], P(('doc', 'resp', 'prob')), may hold values from -6 to 6
- lengths: int32 [128], P(('doc', 'resp', 'prob')), may hold values from 64 to 128, as said below
Outputs:
- grad_queries: bfloat16 [128, 128, 4096], P(('doc', 'resp', 'prob'))
- grad_keys: bfloat16 [128, 128, 512], P(('doc', 'resp', 'prob'))
- grad_values: bfloat16 [128, 128, 512], P(('doc', 'resp', 'prob'))
- grad_doc: bfloat16 [512, 5120], P('doc')
- grad_prompt: bfloat16 [4, 1024, 5120], P('prob', 'resp')
Inputs may be any that keep to these rules, and one draw needn't show every extreme that they name: `lengths`: token slots at or beyond a response's length are padding.
All inputs are finite; a program needn't handle non-finite values.
Results may differ from a plain program's by a relative error of at most 0.0085.
Values may be sent and summed in bfloat16 or wider, within the bound.
No kernel may reach another device: no remote copies, remote signals or barrier semaphores. Data moves between devices by JAX's collectives and lax.ppermute only.
A program may use at most 128 MiB of HBM per device.

v0:
```python
import jax
import jax.numpy as jnp
import numpy as np
from jax import lax
from jax.experimental import pallas as pl
from jax.experimental.pallas import tpu as pltpu
from jax.sharding import PartitionSpec as P

D = 5120
QH = 32
KVH = 4
HD = 128
R = 128
GROUP = QH // KVH
WIDE = GROUP * HD
KVW = 2 * HD
NZ = 4
DOC = 512
PROMPT = 1024
PRE = DOC + PROMPT
KEYS = PRE + R
SCALE = 1.0 / HD**0.5
LOG2E = 1.4426950408889634
MSG = 2 * WIDE + KVW + HD
RET = WIDE + KVW
BF = jnp.bfloat16
F32 = jnp.float32
TILE = 1024
VMEM = pl.BlockSpec(memory_space=pltpu.VMEM)
SMEM = pl.BlockSpec(memory_space=pltpu.SMEM)
ANY = pl.BlockSpec(memory_space=pl.ANY)


def live_block(length):
    rows = lax.broadcasted_iota(jnp.int32, (R, HD), 0)
    return jnp.where(rows < length, 1.0, 0.0).astype(BF)


def project_kernel(
    length, xd, xp, wk, wv, q, cot, rk, rv, msg_p, msg_m, msg_2, doc_0, doc_1, doc_2, own,
    xs, ws, qs, gs, ks, vs, acc, sems,
):
    y = lax.axis_index("doc")
    first = [
        pltpu.make_async_copy(xd, xs.at[pl.ds(0, R)], sems.at[0]),
        pltpu.make_async_copy(xp.at[0], xs.at[pl.ds(R, R)], sems.at[1]),
    ]
    parts = []
    for i in range(D // TILE):
        rows = pl.ds(i * TILE, TILE)
        parts.append(
            [
                pltpu.make_async_copy(wk.at[rows], ws.at[0, rows], sems.at[6 + 2 * i]),
                pltpu.make_async_copy(wv.at[rows], ws.at[1, rows], sems.at[7 + 2 * i]),
            ]
        )
    rest = [
        pltpu.make_async_copy(a.at[0], b, sems.at[2 + i])
        for i, (a, b) in enumerate(((q, qs), (cot, gs), (rk, ks), (rv, vs)))
    ]
    for c in first + sum(parts, []) + rest:
        c.start()
    for c in first:
        c.wait()
    for i, part_copies in enumerate(parts):
        for c in part_copies:
            c.wait()
        rows = slice(i * TILE, (i + 1) * TILE)
        x = xs[:, rows]
        for k in range(2):
            cols = slice(k * KVH * HD, (k + 1) * KVH * HD)
            term = jnp.dot(x, ws[k, rows, :], preferred_element_type=F32)
            acc[:, cols] = term if i == 0 else acc[:, cols] + term

    def head_pair(row, head):
        at = pl.multiple_of(head * HD, 128)
        return jnp.concatenate(
            [acc[row : row + R, pl.ds(at, HD)], acc[row : row + R, pl.ds(KVH * HD + at, HD)]], axis=1
        ).astype(BF)

    own[...] = head_pair(R, y)
    core = lax.rem(lax.axis_index("prob"), 2)
    for step, doc in ((0, doc_0), (1 + 2 * core, doc_1), (2, doc_2)):
        doc[...] = head_pair(0, lax.rem(y + step, 4))
    for c in rest:
        c.wait()
    live = live_block(length[0])
    for step, msg in ((1, msg_p), (3, msg_m), (2, msg_2)):
        head = lax.rem(y + step, 4)
        wide = pl.ds(pl.multiple_of(head * WIDE, 128), WIDE)
        thin = pl.ds(pl.multiple_of(head * HD, 128), HD)
        msg[:, :WIDE] = qs[:, wide]
        msg[:, WIDE : 2 * WIDE] = gs[:, wide]
        msg[:, 2 * WIDE : 2 * WIDE + HD] = ks[:, thin]
        msg[:, 2 * WIDE + HD : 2 * WIDE + KVW] = vs[:, thin]
        msg[:, MSG - HD : MSG] = live


def project(length, x_doc, x_prompt, w_key, w_value, q, cot, rk, rv):
    out = jax.ShapeDtypeStruct
    return pl.pallas_call(
        project_kernel,
        out_shape=(
            out((R, MSG), BF),
            out((R, MSG), BF),
            out((R, MSG), BF),
            out((R, KVW), BF),
            out((R, KVW), BF),
            out((R, KVW), BF),
            out((R, KVW), BF),
        ),
        in_specs=[SMEM] + [ANY] * 8,
        out_specs=[VMEM] * 7,
        scratch_shapes=[
            pltpu.VMEM((2 * R, D), BF),
            pltpu.VMEM((2, D, KVH * HD), BF),
            pltpu.VMEM((R, QH * HD), BF),
            pltpu.VMEM((R, QH * HD), BF),
            pltpu.VMEM((R, KVH * HD), BF),
            pltpu.VMEM((R, KVH * HD), BF),
            pltpu.VMEM((2 * R, 2 * KVH * HD), F32),
            pltpu.SemaphoreType.DMA((6 + 2 * (D // TILE),)),
        ],
        compiler_params=pltpu.CompilerParams(vmem_limit_bytes=56 * 2**20),
        cost_estimate=pl.CostEstimate(flops=2 * 256 * D * 1024, bytes_accessed=18 * 2**20, transcendentals=0),
        name="project",
    )(length, x_doc, x_prompt, w_key, w_value, q, cot, rk, rv)


CHUNK = 256
FIRST_COST = 5 * 10**9
MID_COST = 10**10
LAST_COST = 5 * 10**9


def attend_one(q_of, g_of, own, live, kv, key_t, before, acc, own_acc, ret, scores, dprobs):
    own_t = own[:, :HD].T
    key_row = lax.broadcasted_iota(jnp.int32, (R, R), 0)
    query_col = lax.broadcasted_iota(jnp.int32, (R, R), 1)
    allowed = (key_row <= query_col) & live
    allowed = jnp.concatenate([allowed, allowed], axis=1)
    chunks = [(i, CHUNK) for i in range(0, PRE, CHUNK)] + [(PRE, R)]

    def keys_of(start, size):
        return own[:, :HD] if start == PRE else kv[start : start + size, :HD]

    def values_of(start, size):
        return own[:, HD:] if start == PRE else kv[start : start + size, HD:]

    state = {}

    def prepare(j):
        two_q, two_g = q_of(j), g_of(j)
        nought = jnp.zeros((R, HD), BF)
        q0, q1 = two_q[:, :HD], two_q[:, HD:]
        g0 = jnp.where(live, two_g[:, :HD], nought)
        g1 = jnp.where(live, two_g[:, HD:], nought)
        state[j] = dict(
            q_rows=jnp.concatenate([q0, q1], axis=0),
            g_rows=jnp.concatenate([g0, g1], axis=0),
            q_t=jnp.concatenate([q0.T, q1.T], axis=1),
            g_t=jnp.concatenate([g0.T, g1.T], axis=1),
            peak=None,
            total=jnp.zeros((1, KVW), F32),
            delta=jnp.zeros((1, KVW), F32),
            dq_t=jnp.zeros((HD, KVW), F32),
        )

    def step_a(j, start, size):
        st = state[j]
        s = jnp.dot(keys_of(start, size), st["q_t"], preferred_element_type=F32)
        if start == PRE:
            s = jnp.where(allowed, s, -1e30)
        scores[j % 2, start : start + size, :] = s
        top = jnp.max(s, axis=0, keepdims=True)
        st["peak"] = top if st["peak"] is None else jnp.maximum(st["peak"], top)

    def step_b(j, start, size):
        st = state[j]
        rows = slice(start, start + size)
        e = jnp.exp2(scores[j % 2, rows, :] * (SCALE * LOG2E) - st["shift"])
        dp = jnp.dot(values_of(start, size), st["g_t"], preferred_element_type=F32)
        st["total"] += jnp.sum(e, axis=0, keepdims=True)
        st["delta"] += jnp.sum(e * dp, axis=0, keepdims=True)
        scores[j % 2, rows, :] = e
        dprobs[j % 2, rows, :] = dp

    def step_c(j, start, size):
        st = state[j]
        rows = slice(start, start + size)
        p = scores[j % 2, rows, :] * st["inv"]
        ds = (p * (dprobs[j % 2, rows, :] - st["delta"])).astype(BF)
        dk = jnp.dot(ds, st["q_rows"], preferred_element_type=F32)
        dv = jnp.dot(p.astype(BF), st["g_rows"], preferred_element_type=F32)
        if start == PRE:
            where, old = own_acc, own_acc if j else None
            rows = slice(0, R)
            left = own_t
        else:
            where, old = acc, acc if j else before
            left = key_t[:, rows]
        where[rows, :HD] = dk if old is None else old[rows, :HD] + dk
        where[rows, HD:] = dv if old is None else old[rows, HD:] + dv
        st["dq_t"] += jnp.dot(left, ds, preferred_element_type=F32)

    def end_a(j):
        state[j]["shift"] = state[j]["peak"] * (SCALE * LOG2E)

    def end_b(j):
        state[j]["inv"] = 1.0 / state[j]["total"]
        state[j]["delta"] = state[j]["delta"] * state[j]["inv"]

    def end_c(j):
        dq_t = state[j]["dq_t"] * SCALE
        ret[:, j * KVW : (j + 1) * KVW] = jnp.concatenate([dq_t[:, :HD].T, dq_t[:, HD:].T], axis=1).astype(BF)

    last = GROUP // 2 - 1
    prepare(0)
    for c in chunks:
        step_a(0, *c)
    end_a(0)
    for j in range(GROUP // 2):
        if j < last:
            prepare(j + 1)
        for c in chunks:
            step_b(j, *c)
            if j < last:
                step_a(j + 1, *c)
        end_b(j)
        if j < last:
            end_a(j + 1)
        for c in chunks:
            step_c(j, *c)
        end_c(j)
    ret[:, WIDE:] = scaled(own_acc[...])


def scaled(block):
    col = lax.broadcasted_iota(jnp.int32, block.shape, 1)
    return (block * jnp.where(col < HD, SCALE, 1.0)).astype(BF)


def attend_bundle(msg, *rest):
    def q_of(j):
        return msg[:, j * KVW : (j + 1) * KVW]

    def g_of(j):
        return msg[:, WIDE + j * KVW : WIDE + (j + 1) * KVW]

    own = msg[:, 2 * WIDE : 2 * WIDE + KVW]
    attend_one(q_of, g_of, own, msg[:, MSG - HD :] > 0, *rest)


def attend_first_kernel(
    length, q, cot, rk, rv, doc_0, mine, other, doc_2, z0, z1, z2, z3,
    ret, kv, key_t, acc, own_acc, scores, dprobs,
):
    core = lax.rem(lax.axis_index("prob"), 2)
    for row, piece in ((0, doc_0), (3 - 2 * core, mine), (1 + 2 * core, other), (2, doc_2)):
        kv[pl.ds(pl.multiple_of(row * R, R), R), :] = piece[...]
    for k, block in enumerate((z0, z1, z2, z3)):
        kv[DOC + 2 * R * k : DOC + 2 * R * (k + 1), :] = block[...]
    key_t[...] = kv[:, :HD].T
    head = lax.axis_index("doc")

    def q_of(j):
        return q[0, :, pl.ds(pl.multiple_of(head * WIDE + j * KVW, 128), KVW)]

    def g_of(j):
        return cot[0, :, pl.ds(pl.multiple_of(head * WIDE + j * KVW, 128), KVW)]

    thin = pl.ds(pl.multiple_of(head * HD, 128), HD)
    own = jnp.concatenate([rk[0, :, thin], rv[0, :, thin]], axis=1)
    live = live_block(length[0]) > 0
    attend_one(q_of, g_of, own, live, kv, key_t, None, acc, own_acc, ret, scores, dprobs)


def attend_mid_kernel(msg_m, msg_p, kv, key_t, before, ret_m, ret_p, acc, own_acc, scores, dprobs):
    attend_bundle(msg_m, kv, key_t, before, acc, own_acc, ret_m, scores, dprobs)
    attend_bundle(msg_p, kv, key_t, acc, acc, own_acc, ret_p, scores, dprobs)


def attend_last_kernel(msg_2, kv, key_t, before, ret_2, m0, m1, m2, m3, acc, own_acc, scores, dprobs):
    attend_bundle(msg_2, kv, key_t, before, acc, own_acc, ret_2, scores, dprobs)
    y, z = lax.axis_index("doc"), lax.axis_index("resp") // 2
    for k, out in enumerate((m0, m1, m2, m3)):
        rows = pl.ds(pl.multiple_of(lax.rem(z + k - y + 4, 4) * R, R), R)
        out[:R] = scaled(acc[rows, :])
        out[R:] = scaled(acc[DOC + 2 * R * k : DOC + 2 * R * (k + 1), :])


RET_SHAPE = jax.ShapeDtypeStruct((R, RET), BF)
ACC_SHAPE = jax.ShapeDtypeStruct((PRE, KVW), F32)


def attend(kernel, name, count, in_specs, outs, scratch, *args):
    return pl.pallas_call(
        kernel,
        out_shape=outs,
        in_specs=in_specs,
        out_specs=[VMEM] * len(outs),
        scratch_shapes=scratch
        + [pltpu.VMEM((R, KVW), F32), pltpu.VMEM((2, KEYS, KVW), F32), pltpu.VMEM((2, KEYS, KVW), F32)],
        compiler_params=pltpu.CompilerParams(vmem_limit_bytes=24 * 2**20),
        cost_estimate=pl.CostEstimate(
            flops=count, bytes_accessed=0, transcendentals=0
        ),
        name=name,
    )(*args)


def attend_first(length, q, cot, rk, rv, docs, zs):
    out = jax.ShapeDtypeStruct
    outs = [RET_SHAPE, out((PRE, KVW), BF), out((HD, PRE), BF), ACC_SHAPE]
    specs = [SMEM] + [VMEM] * 12
    return attend(attend_first_kernel, "attend_first", FIRST_COST, specs, outs, [], length, q, cot, rk, rv, *docs, *zs)


def attend_mid(msg_m, msg_p, kv, key_t, acc):
    outs = [RET_SHAPE, RET_SHAPE, ACC_SHAPE]
    return attend(attend_mid_kernel, "attend_mid", MID_COST, [VMEM] * 5, outs, [], msg_m, msg_p, kv, key_t, acc)


def attend_last(msg_2, kv, key_t, acc):
    outs = [RET_SHAPE] + [jax.ShapeDtypeStruct((3 * R, KVW), BF)] * 4
    scratch = [pltpu.VMEM((PRE, KVW), F32)]
    return attend(attend_last_kernel, "attend_last", LAST_COST, [VMEM] * 4, outs, scratch, msg_2, kv, key_t, acc)


def unpack_kernel(r0, r1, r2, r3, gq, gk, gv):
    for k, r in enumerate((r0, r1, r2, r3)):
        head = lax.rem(lax.axis_index("doc") + k, 4)
        thin = pl.ds(pl.multiple_of(head * HD, 128), HD)
        gq[0, :, pl.ds(pl.multiple_of(head * WIDE, 128), WIDE)] = r[:, :WIDE]
        gk[0, :, thin] = r[:, WIDE : WIDE + HD]
        gv[0, :, thin] = r[:, WIDE + HD :]


def unpack(rets):
    out = jax.ShapeDtypeStruct
    return pl.pallas_call(
        unpack_kernel,
        out_shape=(out((1, R, QH * HD), BF), out((1, R, KVH * HD), BF), out((1, R, KVH * HD), BF)),
        in_specs=[VMEM] * 4,
        out_specs=[VMEM] * 3,
        compiler_params=pltpu.CompilerParams(vmem_limit_bytes=12 * 2**20),
        cost_estimate=pl.CostEstimate(flops=0, bytes_accessed=2**22, transcendentals=0),
        name="unpack",
    )(*rets)


def finish_kernel(d0, d1, d2, d3, p0, p1, p2, p3, wk, wv, grad_doc, grad_prompt, left, out, sems):
    y, z, core = lax.axis_index("doc"), lax.axis_index("resp") // 2, lax.axis_index("prob") % 2
    for k, (doc, prompt) in enumerate(((d0, p0), (d1, p1), (d2, p2), (d3, p3))):
        step = lax.rem(2 * core + k, 4)
        for row, piece, head in ((0, doc, lax.rem(z + 4 - step, 4)), (R, prompt, lax.rem(y + k, 4))):
            at = pl.multiple_of(head * HD, 128)
            left[row : row + R, pl.ds(at, HD)] = piece[:, :HD]
            left[row : row + R, pl.ds(KVH * HD + at, HD)] = piece[:, HD:]
    over = (((1,), (1,)), ((), ()))
    copies = []
    for i in range(D // TILE):
        cols = slice(i * TILE, (i + 1) * TILE)
        total = lax.dot_general(left[:, : KVH * HD], wk[cols, :], over, preferred_element_type=F32)
        total += lax.dot_general(left[:, KVH * HD :], wv[cols, :], over, preferred_element_type=F32)
        out[:, cols] = total.astype(BF)
        cols = pl.ds(i * TILE, TILE)
        copies += [
            pltpu.make_async_copy(out.at[pl.ds(0, R), cols], grad_doc.at[:, cols], sems.at[2 * i]),
            pltpu.make_async_copy(out.at[pl.ds(R, R), cols], grad_prompt.at[0, :, cols], sems.at[2 * i + 1]),
        ]
        copies[-2].start()
        copies[-1].start()
    for c in copies:
        c.wait()


def finish(docs, prompts, w_key, w_value):
    out = jax.ShapeDtypeStruct
    return pl.pallas_call(
        finish_kernel,
        out_shape=(out((R, D), BF), out((1, R, D), BF)),
        in_specs=[VMEM] * 10,
        out_specs=[ANY, ANY],
        scratch_shapes=[
            pltpu.VMEM((2 * R, 2 * KVH * HD), BF),
            pltpu.VMEM((2 * R, D), BF),
            pltpu.SemaphoreType.DMA((2 * (D // TILE),)),
        ],
        compiler_params=pltpu.CompilerParams(vmem_limit_bytes=20 * 2**20),
        cost_estimate=pl.CostEstimate(flops=2 * 256 * D * 1024, bytes_accessed=18 * 2**20, transcendentals=0),
        name="finish",
    )(*docs, *prompts, w_key, w_value)


def moves(axes, rule):
    sizes = [lax.axis_size(a) for a in axes]
    pairs = []
    for index in range(np.prod(sizes)):
        here = np.unravel_index(index, sizes)
        there = rule(*(int(i) for i in here))
        pairs.append((index, int(np.ravel_multi_index(there, sizes))))
    return (axes if len(axes) > 1 else axes[0]), pairs


def send(x, move):
    return lax.ppermute(x, *move)


def along_y(k):
    return moves(("doc",), lambda y: ((y + k) % 4,))


def turned(resp, k):
    return ((resp // 2 + k) % NZ) * 2 + resp % 2


def beside_y():
    return moves(("doc", "prob"), lambda y, p: ((y + 1 + 2 * (p % 2)) % 4, p))


def along_z(k):
    return moves(("resp",), lambda r: (turned(r, k),))


def along_x(k):
    def rule(resp, prob):
        x = ((resp % 2) * 2 + prob // 2 + k) % 4
        return (resp // 2) * 2 + x // 2, (x % 2) * 2 + prob % 2

    return moves(("resp", "prob"), rule)


def other_half():
    return moves(("resp",), lambda r: (r ^ 1,))


def other_core():
    return moves(("prob",), lambda p: (p ^ 1,))


def cross(first, second):
    def rule(y, resp, prob):
        k = first if prob % 2 == 0 else second
        return resp // 2, ((y + k) % 4) * 2 + resp % 2, prob

    return moves(("doc", "resp", "prob"), rule)


def added(*pieces):
    total = pieces[0].astype(F32)
    for piece in pieces[1:]:
        total = total + piece.astype(F32)
    return total


def sum_kernel(m0, m1, m2, m3, doc, keep, give):
    total = added(m0[...], m1[...], m2[...], m3[...])
    doc[...] = total[:R].astype(BF)
    keep[...] = total[R : 2 * R]
    give[...] = total[2 * R :].astype(BF)


def sum_blocks(blocks):
    out = jax.ShapeDtypeStruct
    return pl.pallas_call(
        sum_kernel,
        out_shape=(out((R, KVW), BF), out((R, KVW), F32), out((R, KVW), BF)),
        in_specs=[VMEM] * 4,
        out_specs=[VMEM] * 3,
        compiler_params=pltpu.CompilerParams(vmem_limit_bytes=8 * 2**20),
        cost_estimate=pl.CostEstimate(flops=2**18, bytes_accessed=2**20, transcendentals=0),
        name="sum_blocks",
    )(*blocks)


def on_device(x_doc, x_prompt, w_key, w_value, queries, resp_keys, resp_values, out_grad, lengths):
    msg_p, msg_m, msg_2, doc_0, doc_1, doc_2, own = project(
        lengths, x_doc, x_prompt, w_key, w_value, queries, out_grad, resp_keys, resp_values
    )
    half = send(own, other_half())
    doc_1 = send(doc_1, beside_y())
    doc_2 = send(doc_2, along_y(2))
    half, doc_2 = lax.optimization_barrier((half, doc_2))
    docs = [doc_0, doc_1, send(doc_1, other_core()), doc_2]
    block = jnp.concatenate([own, half], axis=0)
    blocks = [block] + [send(block, along_z(-k)) for k in (1, 2, 3)]
    msg_p = send(msg_p, along_y(1))
    msg_m = send(msg_m, along_y(-1))
    msg_2 = send(msg_2, along_y(2))
    ret_0, kv, key_t, acc = attend_first(
        lengths, queries, out_grad, resp_keys, resp_values, docs, blocks
    )
    ret_m, ret_p, acc = attend_mid(msg_m, msg_p, kv, key_t, acc)
    ret_1 = send(ret_p, along_y(-1))
    ret_3 = send(ret_m, along_y(1))
    ret_2, *terms = attend_last(msg_2, kv, key_t, acc)
    ret_2 = send(ret_2, along_y(2))
    blocks = [terms[0]] + [send(terms[k], along_z(k)) for k in (1, 2, 3)]
    blocks, ret_1, ret_3 = lax.optimization_barrier((blocks, ret_1, ret_3))
    doc, keep, give = sum_blocks(blocks)
    doc = added(doc, send(doc, other_core())).astype(BF)
    doc = added(doc, *(send(doc, along_x(k)) for k in (1, 2, 3))).astype(BF)
    prompt = added(keep, send(give, other_half())).astype(BF)
    doc, ret_2 = lax.optimization_barrier((doc, ret_2))
    mine = [send(doc, cross(0, 2)), send(doc, cross(1, 3))]
    docs = mine + [send(piece, other_core()) for piece in mine]
    prompts = [prompt] + [send(prompt, along_y(-k)) for k in (1, 2, 3)]
    gq, gk, gv = unpack([ret_0, ret_1, ret_2, ret_3])
    grad_doc, grad_prompt = finish(docs, prompts, w_key, w_value)
    return gq, gk, gv, grad_doc, grad_prompt


def solution(mesh):
    placed = (
        P("doc", None),
        P("prob", "resp", None),
        P(),
        P(),
        P(("doc", "resp", "prob"), None, None),
        P(("doc", "resp", "prob"), None, None),
        P(("doc", "resp", "prob"), None, None),
        P(("doc", "resp", "prob"), None, None),
        P(("doc", "resp", "prob")),
    )
    return jax.shard_map(
        on_device,
        mesh=mesh,
        in_specs=placed,
        out_specs=(
            P(("doc", "resp", "prob"), None, None),
            P(("doc", "resp", "prob"), None, None),
            P(("doc", "resp", "prob"), None, None),
            P("doc", None),
            P("prob", "resp", None),
        ),
        check_vma=False,
    )
```

profile of v0, /device:TPU:0, one launch (start us, length us, event | category | flops | bytes accessed | tf_op | source)
XLA Modules:
  0.0 117.9 jit_solution(13370480084023958007)
XLA Ops:
  1.3 7.3 %project.1 = (bf16[128,2432]{1,0:T(8,128)(2,1)}, bf16[128,2432]{1,0:T(8,128)(2,1)}, bf16[128,2432]{1,0:T(8,128)(2,1)}, bf16[128,256]{1,0:T(8,128)(2,1)}, bf16[12...) custom-call(s32[1]{0:T(128)S(6)} %copy.15.length, bf16[128,5120]{1,0:T(8,128)(2,1)} %xd.1, ...), custom_call_target="tpu_custom_call" | custom-call | flops 2684354560 | bytes 18874368 | tf_op jit(solution)/shard_map/project/pallas_call | solution.py:101
  8.6 1.7 %collective-permute-start = (bf16[128,256]{1,0:T(8,128)(2,1)}, bf16[128,256]{1,0:T(8,128)(2,1)S(1)}, u32[]{:S(2)}, u32[]{:S(2)}) collective-permute-start(bf16[128,256]{1,0:T(8,128)(2,1)} %get-tuple-element.43), channel_id=1, source_target_pairs={{0,32},{1,97},{2,34},{3,99},{32,64},{33,1},{34,66},{35,3},{64,96},... | collective-permute-start | bytes 196616 | tf_op jit(solution)/shard_map/ppermute | solution.py:407
  10.4 2.9 %collective-permute-start.3 = (bf16[128,256]{1,0:T(8,128)(2,1)}, bf16[128,256]{1,0:T(8,128)(2,1)S(1)}, u32[]{:S(2)}, u32[]{:S(2)}) collective-permute-start(bf16[128,256]{1,0:T(8,128)(2,1)} %get-tuple-element.45), channel_id=1, source_target_pairs={{0,64},{32,96},{64,0},{96,32},{1,65},{33,97},{65,1},{97,33},{2,66}... | collective-permute-start | bytes 196616 | tf_op jit(solution)/shard_map/ppermute | solution.py:407
  13.3 3.0 %collective-permute-start.2 = (bf16[128,256]{1,0:T(8,128)(2,1)}, bf16[128,256]{1,0:T(8,128)(2,1)S(1)}, u32[]{:S(2)}, u32[]{:S(2)}) collective-permute-start(bf16[128,256]{1,0:T(8,128)(2,1)} %get-tuple-element.44), channel_id=1, source_target_pairs={{0,4},{4,0},{8,12},{12,8},{16,20},{20,16},{24,28},{28,24},{1,5},{5... | collective-permute-start | bytes 196616 | tf_op jit(solution)/shard_map/ppermute | solution.py:407
  16.3 1.3 %collective-permute-start.8 = (bf16[128,2432]{1,0:T(8,128)(2,1)}, bf16[128,2432]{1,0:T(8,128)(2,1)S(1)}, u32[]{:S(2)}, u32[]{:S(2)}) collective-permute-start(bf16[128,2432]{1,0:T(8,128)(2,1)} %get-tuple-element.52), channel_id=1, source_target_pairs={{0,96},{32,0},{64,32},{96,64},{1,97},{33,1},{65,33},{97,65},{2,98}... | collective-permute-start | bytes 1867784 | tf_op jit(solution)/shard_map/ppermute | solution.py:407
  19.3 2.0 %collective-permute-start.6 = (bf16[256,256]{1,0:T(8,128)(2,1)S(1)}, bf16[256,256]{1,0:T(8,128)(2,1)S(1)}, u32[]{:S(2)}, u32[]{:S(2)}) collective-permute-start(bf16[256,256]{1,0:T(8,128)(2,1)S(1)} %constant_dynamic-update-slice_fusion.z0), channel_id=1, source_target_pairs={{0,8},{4,12},{8,16},{12,20},{16,24},{20,28},{24,0},{28,4},{1,9},{5... | collective-permute-start | bytes 393224 | tf_op jit(solution)/shard_map/ppermute | solution.py:407
  21.3 3.6 %collective-permute-start.5 = (bf16[256,256]{1,0:T(8,128)(2,1)S(1)}, bf16[256,256]{1,0:T(8,128)(2,1)S(1)}, u32[]{:S(2)}, u32[]{:S(2)}) collective-permute-start(bf16[256,256]{1,0:T(8,128)(2,1)S(1)} %constant_dynamic-update-slice_fusion.z0), channel_id=1, source_target_pairs={{0,16},{4,20},{8,24},{12,28},{16,0},{20,4},{24,8},{28,12},{1,17},{... | collective-permute-start | bytes 393224 | tf_op jit(solution)/shard_map/ppermute | solution.py:407
  25.9 1.6 %collective-permute-done.6.z3 = bf16[256,256]{1,0:T(8,128)(2,1)S(1)} collective-permute-done((bf16[256,256]{1,0:T(8,128)(2,1)S(1)}, bf16[256,256]{1,0:T(8,128)(2,1)S(1)}, u32[]{:S(2)}, u32[]{:S(2)}) %collective-permute-start.6) | collective-permute-done | bytes 131104 | tf_op jit(solution)/shard_map/ppermute | solution.py:407
  27.5 1.3 %collective-permute-start.7 = (bf16[128,2432]{1,0:T(8,128)(2,1)}, bf16[128,2432]{1,0:T(8,128)(2,1)S(1)}, u32[]{:S(2)}, u32[]{:S(2)}) collective-permute-start(bf16[128,2432]{1,0:T(8,128)(2,1)} %get-tuple-element.49), channel_id=1, source_target_pairs={{0,64},{32,96},{64,0},{96,32},{1,65},{33,97},{65,1},{97,33},{2,66}... | collective-permute-start | bytes 1867784 | tf_op jit(solution)/shard_map/ppermute | solution.py:407
  28.8 2.7 %collective-permute-done.5.z2 = bf16[256,256]{1,0:T(8,128)(2,1)S(1)} collective-permute-done((bf16[256,256]{1,0:T(8,128)(2,1)S(1)}, bf16[256,256]{1,0:T(8,128)(2,1)S(1)}, u32[]{:S(2)}, u32[]{:S(2)}) %collective-permute-start.5) | collective-permute-done | bytes 131104 | tf_op jit(solution)/shard_map/ppermute | solution.py:407
  32.3 6.0 %attend_first.1 = (bf16[128,1280]{1,0:T(8,128)(2,1)S(1)}, bf16[1536,256]{1,0:T(8,128)(2,1)S(1)}, bf16[128,1536]{1,0:T(8,128)(2,1)S(1)}, f32[1536,256]{1,0:T(8,128)S(1)}) custom-call(s32[1]{0:T(128)S(6)} %copy.15.length, bf16[1,128,4096]{2,1,0:T(8,128)(2,1)S(1)} %copy-done, bf16[1,128,4096]{2,1,0:T(8,128)(2,1)S(1)} %copy-done.1, ...), custom_call_target="tpu_custom_call" | custom-call | flops 5000000000 | tf_op jit(solution)/shard_map/attend_first/pallas_call | solution.py:297
  38.4 25.8 %attend_mid.1 = (bf16[128,1280]{1,0:T(8,128)(2,1)S(1)}, bf16[128,1280]{1,0:T(8,128)(2,1)S(1)}, f32[1536,256]{1,0:T(8,128)S(1)}) custom-call(bf16[128,2432]{1,0:T(8,128)(2,1)S(1)} %collective-permute-done.8.msg_m, bf16[128,2432]{1,0:T(8,128)(2,1)S(1)} %collective-permute-done.9.msg_p, bf16[1536,256]{1,0:T(8,128)(2,1)S(1)} %get-tuple-element.50.kv, ...), custom_call_target="tpu_custom_call" | custom-call | flops 10000000000 | tf_op jit(solution)/shard_map/attend_mid/pallas_call | solution.py:297
  64.2 2.6 %collective-permute-start.13 = (bf16[128,1280]{1,0:T(8,128)(2,1)S(1)}, bf16[128,1280]{1,0:T(8,128)(2,1)S(1)}, u32[]{:S(2)}, u32[]{:S(2)}) collective-permute-start(bf16[128,1280]{1,0:T(8,128)(2,1)S(1)} %get-tuple-element.60), channel_id=1, source_target_pairs={{0,96},{32,0},{64,32},{96,64},{1,97},{33,1},{65,33},{97,65},{2,98}... | collective-permute-start | bytes 983048 | tf_op jit(solution)/shard_map/ppermute | solution.py:407
  66.8 6.1 %attend_last.1 = (bf16[128,1280]{1,0:T(8,128)(2,1)S(1)}, bf16[384,256]{1,0:T(8,128)(2,1)S(1)}, bf16[384,256]{1,0:T(8,128)(2,1)S(1)}, bf16[384,256]{1,0:T(8,128)(2,1)S(1)}, bf16[384,256]{1,0:T(8,128)(2,1)S(1)}) custom-call(bf16[128,2432]{1,0:T(8,128)(2,1)S(1)} %collective-permute-done.7.msg_2, bf16[1536,256]{1,0:T(8,128)(2,1)S(1)} %get-tuple-element.50.kv, ...), custom_call_target="tpu_custom_call" | custom-call | flops 5000000000 | tf_op jit(solution)/shard_map/attend_last/pallas_call | solution.py:297
  72.9 1.3 %collective-permute-start.10 = (bf16[384,256]{1,0:T(8,128)(2,1)S(1)}, bf16[384,256]{1,0:T(8,128)(2,1)S(1)}, u32[]{:S(2)}, u32[]{:S(2)}) collective-permute-start(bf16[384,256]{1,0:T(8,128)(2,1)S(1)} %get-tuple-element.57), channel_id=1, source_target_pairs={{0,8},{4,12},{8,16},{12,20},{16,24},{20,28},{24,0},{28,4},{1,9},{5... | collective-permute-start | bytes 589832 | tf_op jit(solution)/shard_map/ppermute | solution.py:407
  74.2 2.4 %collective-permute-start.11 = (bf16[384,256]{1,0:T(8,128)(2,1)S(1)}, bf16[384,256]{1,0:T(8,128)(2,1)S(1)}, u32[]{:S(2)}, u32[]{:S(2)}) collective-permute-start(bf16[384,256]{1,0:T(8,128)(2,1)S(1)} %get-tuple-element.58), channel_id=1, source_target_pairs={{0,16},{4,20},{8,24},{12,28},{16,0},{20,4},{24,8},{28,12},{1,17},{... | collective-permute-start | bytes 589832 | tf_op jit(solution)/shard_map/ppermute | solution.py:407
  76.6 1.2 %collective-permute-start.12 = (bf16[384,256]{1,0:T(8,128)(2,1)S(1)}, bf16[384,256]{1,0:T(8,128)(2,1)S(1)}, u32[]{:S(2)}, u32[]{:S(2)}) collective-permute-start(bf16[384,256]{1,0:T(8,128)(2,1)S(1)} %get-tuple-element.59), channel_id=1, source_target_pairs={{0,24},{4,28},{8,0},{12,4},{16,8},{20,12},{24,16},{28,20},{1,25},{... | collective-permute-start | bytes 589832 | tf_op jit(solution)/shard_map/ppermute | solution.py:407
  77.9 3.1 %collective-permute-done.10.m1 = bf16[384,256]{1,0:T(8,128)(2,1)S(1)} collective-permute-done((bf16[384,256]{1,0:T(8,128)(2,1)S(1)}, bf16[384,256]{1,0:T(8,128)(2,1)S(1)}, u32[]{:S(2)}, u32[]{:S(2)}) %collective-permute-start.10) | collective-permute-done | bytes 196640 | tf_op jit(solution)/shard_map/ppermute | solution.py:407
  81.0 4.3 %collective-permute-done.11.m2 = bf16[384,256]{1,0:T(8,128)(2,1)S(1)} collective-permute-done((bf16[384,256]{1,0:T(8,128)(2,1)S(1)}, bf16[384,256]{1,0:T(8,128)(2,1)S(1)}, u32[]{:S(2)}, u32[]{:S(2)}) %collective-permute-start.11) | collective-permute-done | bytes 196640 | tf_op jit(solution)/shard_map/ppermute | solution.py:407
  85.5 1.6 %collective-permute-start.19 = (bf16[128,1280]{1,0:T(8,128)(2,1)S(1)}, bf16[128,1280]{1,0:T(8,128)(2,1)S(1)}, u32[]{:S(2)}, u32[]{:S(2)}) collective-permute-start(bf16[128,1280]{1,0:T(8,128)(2,1)S(1)} %get-tuple-element.68), channel_id=1, source_target_pairs={{0,64},{32,96},{64,0},{96,32},{1,65},{33,97},{65,1},{97,33},{2,66}... | collective-permute-start | bytes 983048 | tf_op jit(solution)/shard_map/ppermute | solution.py:407
  87.1 1.6 %collective-permute-start.18 = (bf16[128,256]{1,0:T(8,128)(2,1)S(1)}, bf16[128,256]{1,0:T(8,128)(2,1)S(1)}, u32[]{:S(2)}, u32[]{:S(2)}) collective-permute-start(bf16[128,256]{1,0:T(8,128)(2,1)S(1)} %add_convert_fusion.2), channel_id=1, source_target_pairs={{0,6},{1,7},{2,0},{3,1},{4,2},{5,3},{6,4},{7,5},{8,14},{9,15},{10,... | collective-permute-start | bytes 196616 | tf_op jit(solution)/shard_map/ppermute | solution.py:407
  88.8 1.1 collective-permute-start.17
  90.5 2.9 %collective-permute-start.24 = (bf16[128,256]{1,0:T(8,128)(2,1)S(1)}, bf16[128,256]{1,0:T(8,128)(2,1)S(1)}, u32[]{:S(2)}, u32[]{:S(2)}) collective-permute-start(bf16[128,256]{1,0:T(8,128)(2,1)S(1)} %get-tuple-element.76), channel_id=1, source_target_pairs={{0,4},{4,0},{8,12},{12,8},{16,20},{20,16},{24,28},{28,24},{1,5},{5... | collective-permute-start | bytes 196616 | tf_op jit(solution)/shard_map/ppermute | solution.py:407
  93.4 1.9 %collective-permute-done.17 = bf16[128,256]{1,0:T(8,128)(2,1)S(1)} collective-permute-done((bf16[128,256]{1,0:T(8,128)(2,1)S(1)}, bf16[128,256]{1,0:T(8,128)(2,1)S(1)}, u32[]{:S(2)}, u32[]{:S(2)}) %collective-permute-start.17) | collective-permute-done | bytes 65568 | tf_op jit(solution)/shard_map/ppermute | solution.py:407
  95.3 1.0 collective-permute-done.16
  97.2 1.2 %collective-permute-start.21 = (bf16[128,256]{1,0:T(8,128)(2,1)S(1)}, bf16[128,256]{1,0:T(8,128)(2,1)S(1)}, u32[]{:S(2)}, u32[]{:S(2)}) collective-permute-start(bf16[128,256]{1,0:T(8,128)(2,1)S(1)} %add_convert_fusion.1), channel_id=1, source_target_pairs={{0,8},{1,25},{2,10},{3,27},{4,12},{5,29},{6,14},{7,31},{8,40},{9,5... | collective-permute-start | bytes 196616 | tf_op jit(solution)/shard_map/ppermute | solution.py:407
  99.0 4.4 %collective-permute-start.27 = (bf16[128,256]{1,0:T(8,128)(2,1)S(1)}, bf16[128,256]{1,0:T(8,128)(2,1)S(1)}, u32[]{:S(2)}, u32[]{:S(2)}) collective-permute-start(bf16[128,256]{1,0:T(8,128)(2,1)S(1)} %add_convert_fusion.p0), channel_id=1, source_target_pairs={{0,32},{32,64},{64,96},{96,0},{1,33},{33,65},{65,97},{97,1},{2,34}... | collective-permute-start | bytes 196616 | tf_op jit(solution)/shard_map/ppermute | solution.py:407
  103.4 6.1 %collective-permute-start.26 = (bf16[128,256]{1,0:T(8,128)(2,1)S(1)}, bf16[128,256]{1,0:T(8,128)(2,1)S(1)}, u32[]{:S(2)}, u32[]{:S(2)}) collective-permute-start(bf16[128,256]{1,0:T(8,128)(2,1)S(1)} %add_convert_fusion.p0), channel_id=1, source_target_pairs={{0,64},{32,96},{64,0},{96,32},{1,65},{33,97},{65,1},{97,33},{2,66}... | collective-permute-start | bytes 196616 | tf_op jit(solution)/shard_map/ppermute | solution.py:407
  110.0 1.2 unpack.1
  111.2 1.3 %collective-permute-done.26.p2 = bf16[128,256]{1,0:T(8,128)(2,1)S(1)} collective-permute-done((bf16[128,256]{1,0:T(8,128)(2,1)S(1)}, bf16[128,256]{1,0:T(8,128)(2,1)S(1)}, u32[]{:S(2)}, u32[]{:S(2)}) %collective-permute-start.26) | collective-permute-done | bytes 65568 | tf_op jit(solution)/shard_map/ppermute | solution.py:407
  112.5 1.3 %collective-permute-done.25.p1 = bf16[128,256]{1,0:T(8,128)(2,1)S(1)} collective-permute-done((bf16[128,256]{1,0:T(8,128)(2,1)S(1)}, bf16[128,256]{1,0:T(8,128)(2,1)S(1)}, u32[]{:S(2)}, u32[]{:S(2)}) %collective-permute-start.25) | collective-permute-done | bytes 65568 | tf_op jit(solution)/shard_map/ppermute | solution.py:407
  113.8 3.8 %finish.1 = (bf16[128,5120]{1,0:T(8,128)(2,1)}, bf16[1,128,5120]{2,1,0:T(8,128)(2,1)}) custom-call(bf16[128,256]{1,0:T(8,128)(2,1)S(1)} %collective-permute-done.20.d0, bf16[128,256]{1,0:T(8,128)(2,1)S(1)} %collective-permute-done.21.d1, bf16[128,256]{1,0:T(8,128)(2,1)S(1)} %collective-permute-done.22.d2, bf16[128,256]{1,0:T(8,128)(2,1)S(1)} %collective-permute-done.23.d3, ...), custom_call_target="tpu_custom_call" | custom-call | flops 2684354560 | bytes 18874368 | tf_op jit(solution)/shard_map/finish/pallas_call | solution.py:380
  (56 shorter events, 6.3 us)
Async XLA Ops:
  8.6 10.6 %collective-permute-start = (bf16[128,256]{1,0:T(8,128)(2,1)}, bf16[128,256]{1,0:T(8,128)(2,1)S(1)}, u32[]{:S(2)}, u32[]{:S(2)}) collective-permute-start(bf16[128,256]{1,0:T(8,128)(2,1)} %get-tuple-element.43), channel_id=1, source_target_pairs={{0,32},{1,97},{2,34},{3,99},{32,64},{33,1},{34,66},{35,3},{64,96},... | collective-permute-start | bytes 196616 | tf_op jit(solution)/shard_map/ppermute | solution.py:407
  10.4 8.8 %collective-permute-start.3 = (bf16[128,256]{1,0:T(8,128)(2,1)}, bf16[128,256]{1,0:T(8,128)(2,1)S(1)}, u32[]{:S(2)}, u32[]{:S(2)}) collective-permute-start(bf16[128,256]{1,0:T(8,128)(2,1)} %get-tuple-element.45), channel_id=1, source_target_pairs={{0,64},{32,96},{64,0},{96,32},{1,65},{33,97},{65,1},{97,33},{2,66}... | collective-permute-start | bytes 196616 | tf_op jit(solution)/shard_map/ppermute | solution.py:407
  13.3 6.0 %collective-permute-start.2 = (bf16[128,256]{1,0:T(8,128)(2,1)}, bf16[128,256]{1,0:T(8,128)(2,1)S(1)}, u32[]{:S(2)}, u32[]{:S(2)}) collective-permute-start(bf16[128,256]{1,0:T(8,128)(2,1)} %get-tuple-element.44), channel_id=1, source_target_pairs={{0,4},{4,0},{8,12},{12,8},{16,20},{20,16},{24,28},{28,24},{1,5},{5... | collective-permute-start | bytes 196616 | tf_op jit(solution)/shard_map/ppermute | solution.py:407
  16.3 22.1 %collective-permute-start.8 = (bf16[128,2432]{1,0:T(8,128)(2,1)}, bf16[128,2432]{1,0:T(8,128)(2,1)S(1)}, u32[]{:S(2)}, u32[]{:S(2)}) collective-permute-start(bf16[128,2432]{1,0:T(8,128)(2,1)} %get-tuple-element.52), channel_id=1, source_target_pairs={{0,96},{32,0},{64,32},{96,64},{1,97},{33,1},{65,33},{97,65},{2,98}... | collective-permute-start | bytes 1867784 | tf_op jit(solution)/shard_map/ppermute | solution.py:407
  17.6 20.7 %collective-permute-start.9 = (bf16[128,2432]{1,0:T(8,128)(2,1)}, bf16[128,2432]{1,0:T(8,128)(2,1)S(1)}, u32[]{:S(2)}, u32[]{:S(2)}) collective-permute-start(bf16[128,2432]{1,0:T(8,128)(2,1)} %get-tuple-element.53), channel_id=1, source_target_pairs={{0,32},{32,64},{64,96},{96,0},{1,33},{33,65},{65,97},{97,1},{2,34}... | collective-permute-start | bytes 1867784 | tf_op jit(solution)/shard_map/ppermute | solution.py:407
  19.2 5.6 %collective-permute-start.1 = (bf16[128,256]{1,0:T(8,128)(2,1)S(1)}, bf16[128,256]{1,0:T(8,128)(2,1)S(1)}, u32[]{:S(2)}, u32[]{:S(2)}) collective-permute-start(bf16[128,256]{1,0:T(8,128)(2,1)S(1)} %collective-permute-done.mine), channel_id=1, source_target_pairs={{0,1},{1,0},{2,3},{3,2},{4,5},{5,4},{6,7},{7,6},{8,9},{9,8},{10,11... | collective-permute-start | bytes 196616 | tf_op jit(solution)/shard_map/ppermute | solution.py:407
  19.3 8.2 %collective-permute-start.6 = (bf16[256,256]{1,0:T(8,128)(2,1)S(1)}, bf16[256,256]{1,0:T(8,128)(2,1)S(1)}, u32[]{:S(2)}, u32[]{:S(2)}) collective-permute-start(bf16[256,256]{1,0:T(8,128)(2,1)S(1)} %constant_dynamic-update-slice_fusion.z0), channel_id=1, source_target_pairs={{0,8},{4,12},{8,16},{12,20},{16,24},{20,28},{24,0},{28,4},{1,9},{5... | collective-permute-start | bytes 393224 | tf_op jit(solution)/shard_map/ppermute | solution.py:407
  21.3 10.2 %collective-permute-start.5 = (bf16[256,256]{1,0:T(8,128)(2,1)S(1)}, bf16[256,256]{1,0:T(8,128)(2,1)S(1)}, u32[]{:S(2)}, u32[]{:S(2)}) collective-permute-start(bf16[256,256]{1,0:T(8,128)(2,1)S(1)} %constant_dynamic-update-slice_fusion.z0), channel_id=1, source_target_pairs={{0,16},{4,20},{8,24},{12,28},{16,0},{20,4},{24,8},{28,12},{1,17},{... | collective-permute-start | bytes 393224 | tf_op jit(solution)/shard_map/ppermute | solution.py:407
  24.9 6.6 %collective-permute-start.4 = (bf16[256,256]{1,0:T(8,128)(2,1)S(1)}, bf16[256,256]{1,0:T(8,128)(2,1)S(1)}, u32[]{:S(2)}, u32[]{:S(2)}) collective-permute-start(bf16[256,256]{1,0:T(8,128)(2,1)S(1)} %constant_dynamic-update-slice_fusion.z0), channel_id=1, source_target_pairs={{0,24},{4,28},{8,0},{12,4},{16,8},{20,12},{24,16},{28,20},{1,25},{... | collective-permute-start | bytes 393224 | tf_op jit(solution)/shard_map/ppermute | solution.py:407
  27.5 39.3 %collective-permute-start.7 = (bf16[128,2432]{1,0:T(8,128)(2,1)}, bf16[128,2432]{1,0:T(8,128)(2,1)S(1)}, u32[]{:S(2)}, u32[]{:S(2)}) collective-permute-start(bf16[128,2432]{1,0:T(8,128)(2,1)} %get-tuple-element.49), channel_id=1, source_target_pairs={{0,64},{32,96},{64,0},{96,32},{1,65},{33,97},{65,1},{97,33},{2,66}... | collective-permute-start | bytes 1867784 | tf_op jit(solution)/shard_map/ppermute | solution.py:407
  64.2 21.1 %collective-permute-start.13 = (bf16[128,1280]{1,0:T(8,128)(2,1)S(1)}, bf16[128,1280]{1,0:T(8,128)(2,1)S(1)}, u32[]{:S(2)}, u32[]{:S(2)}) collective-permute-start(bf16[128,1280]{1,0:T(8,128)(2,1)S(1)} %get-tuple-element.60), channel_id=1, source_target_pairs={{0,96},{32,0},{64,32},{96,64},{1,97},{33,1},{65,33},{97,65},{2,98}... | collective-permute-start | bytes 983048 | tf_op jit(solution)/shard_map/ppermute | solution.py:407
  66.8 18.5 %collective-permute-start.14 = (bf16[128,1280]{1,0:T(8,128)(2,1)S(1)}, bf16[128,1280]{1,0:T(8,128)(2,1)S(1)}, u32[]{:S(2)}, u32[]{:S(2)}) collective-permute-start(bf16[128,1280]{1,0:T(8,128)(2,1)S(1)} %get-tuple-element.61), channel_id=1, source_target_pairs={{0,32},{32,64},{64,96},{96,0},{1,33},{33,65},{65,97},{97,1},{2,34}... | collective-permute-start | bytes 983048 | tf_op jit(solution)/shard_map/ppermute | solution.py:407
  66.8 47.0 %slice-start = ((s8[5242880]{0:T(1024)(128)(4,1)}), s8[4194304]{0:T(1024)(128)(4,1)S(1)}, s32[]{:S(2)}) async-start(s8[5242880]{0:T(1024)(128)(4,1)} %bitcast), calls=%async_computation | async-start | bytes 8388608
  66.8 47.0 %slice-start.2 = ((s8[5242880]{0:T(1024)(128)(4,1)}), s8[4194304]{0:T(1024)(128)(4,1)S(1)}, s32[]{:S(2)}) async-start(s8[5242880]{0:T(1024)(128)(4,1)} %bitcast.2), calls=%async_computation.2 | async-start | bytes 8388608
  66.8 47.0 %slice-start.1 = ((s8[5242880]{0:T(1024)(128)(4,1)}), s8[1048576]{0:T(1024)(128)(4,1)S(1)}, s32[]{:S(2)}) async-start(s8[5242880]{0:T(1024)(128)(4,1)} %bitcast), calls=%async_computation.1 | async-start | bytes 2097152
  66.8 47.0 %slice-start.3 = ((s8[5242880]{0:T(1024)(128)(4,1)}), s8[1048576]{0:T(1024)(128)(4,1)S(1)}, s32[]{:S(2)}) async-start(s8[5242880]{0:T(1024)(128)(4,1)} %bitcast.2), calls=%async_computation.3 | async-start | bytes 2097152
  72.9 8.1 %collective-permute-start.10 = (bf16[384,256]{1,0:T(8,128)(2,1)S(1)}, bf16[384,256]{1,0:T(8,128)(2,1)S(1)}, u32[]{:S(2)}, u32[]{:S(2)}) collective-permute-start(bf16[384,256]{1,0:T(8,128)(2,1)S(1)} %get-tuple-element.57), channel_id=1, source_target_pairs={{0,8},{4,12},{8,16},{12,20},{16,24},{20,28},{24,0},{28,4},{1,9},{5... | collective-permute-start | bytes 589832 | tf_op jit(solution)/shard_map/ppermute | solution.py:407
  74.2 11.1 %collective-permute-start.11 = (bf16[384,256]{1,0:T(8,128)(2,1)S(1)}, bf16[384,256]{1,0:T(8,128)(2,1)S(1)}, u32[]{:S(2)}, u32[]{:S(2)}) collective-permute-start(bf16[384,256]{1,0:T(8,128)(2,1)S(1)} %get-tuple-element.58), channel_id=1, source_target_pairs={{0,16},{4,20},{8,24},{12,28},{16,0},{20,4},{24,8},{28,12},{1,17},{... | collective-permute-start | bytes 589832 | tf_op jit(solution)/shard_map/ppermute | solution.py:407
  76.6 8.7 %collective-permute-start.12 = (bf16[384,256]{1,0:T(8,128)(2,1)S(1)}, bf16[384,256]{1,0:T(8,128)(2,1)S(1)}, u32[]{:S(2)}, u32[]{:S(2)}) collective-permute-start(bf16[384,256]{1,0:T(8,128)(2,1)S(1)} %get-tuple-element.59), channel_id=1, source_target_pairs={{0,24},{4,28},{8,0},{12,4},{16,8},{20,12},{24,16},{28,20},{1,25},{... | collective-permute-start | bytes 589832 | tf_op jit(solution)/shard_map/ppermute | solution.py:407
  85.4 1.7 %collective-permute-start.15 = (bf16[128,256]{1,0:T(8,128)(2,1)S(1)}, bf16[128,256]{1,0:T(8,128)(2,1)S(1)}, u32[]{:S(2)}, u32[]{:S(2)}) collective-permute-start(bf16[128,256]{1,0:T(8,128)(2,1)S(1)} %get-tuple-element.67), channel_id=1, source_target_pairs={{0,1},{1,0},{2,3},{3,2},{4,5},{5,4},{6,7},{7,6},{8,9},{9,8},{10,11... | collective-permute-start | bytes 196616 | tf_op jit(solution)/shard_map/ppermute | solution.py:407
  85.5 11.6 %collective-permute-start.19 = (bf16[128,1280]{1,0:T(8,128)(2,1)S(1)}, bf16[128,1280]{1,0:T(8,128)(2,1)S(1)}, u32[]{:S(2)}, u32[]{:S(2)}) collective-permute-start(bf16[128,1280]{1,0:T(8,128)(2,1)S(1)} %get-tuple-element.68), channel_id=1, source_target_pairs={{0,64},{32,96},{64,0},{96,32},{1,65},{33,97},{65,1},{97,33},{2,66}... | collective-permute-start | bytes 983048 | tf_op jit(solution)/shard_map/ppermute | solution.py:407
  87.1 6.2 %collective-permute-start.18 = (bf16[128,256]{1,0:T(8,128)(2,1)S(1)}, bf16[128,256]{1,0:T(8,128)(2,1)S(1)}, u32[]{:S(2)}, u32[]{:S(2)}) collective-permute-start(bf16[128,256]{1,0:T(8,128)(2,1)S(1)} %add_convert_fusion.2), channel_id=1, source_target_pairs={{0,6},{1,7},{2,0},{3,1},{4,2},{5,3},{6,4},{7,5},{8,14},{9,15},{10,... | collective-permute-start | bytes 196616 | tf_op jit(solution)/shard_map/ppermute | solution.py:407
  88.8 6.5 %collective-permute-start.17 = (bf16[128,256]{1,0:T(8,128)(2,1)S(1)}, bf16[128,256]{1,0:T(8,128)(2,1)S(1)}, u32[]{:S(2)}, u32[]{:S(2)}) collective-permute-start(bf16[128,256]{1,0:T(8,128)(2,1)S(1)} %add_convert_fusion.2), channel_id=1, source_target_pairs={{0,4},{1,5},{2,6},{3,7},{4,0},{5,1},{6,2},{7,3},{8,12},{9,13},{10,... | collective-permute-start | bytes 196616 | tf_op jit(solution)/shard_map/ppermute | solution.py:407
  89.9 6.5 %collective-permute-start.16 = (bf16[128,256]{1,0:T(8,128)(2,1)S(1)}, bf16[128,256]{1,0:T(8,128)(2,1)S(1)}, u32[]{:S(2)}, u32[]{:S(2)}) collective-permute-start(bf16[128,256]{1,0:T(8,128)(2,1)S(1)} %add_convert_fusion.2), channel_id=1, source_target_pairs={{0,2},{1,3},{2,4},{3,5},{4,6},{5,7},{6,0},{7,1},{8,10},{9,11},{10,... | collective-permute-start | bytes 196616 | tf_op jit(solution)/shard_map/ppermute | solution.py:407
  90.5 8.5 %collective-permute-start.24 = (bf16[128,256]{1,0:T(8,128)(2,1)S(1)}, bf16[128,256]{1,0:T(8,128)(2,1)S(1)}, u32[]{:S(2)}, u32[]{:S(2)}) collective-permute-start(bf16[128,256]{1,0:T(8,128)(2,1)S(1)} %get-tuple-element.76), channel_id=1, source_target_pairs={{0,4},{4,0},{8,12},{12,8},{16,20},{20,16},{24,28},{28,24},{1,5},{5... | collective-permute-start | bytes 196616 | tf_op jit(solution)/shard_map/ppermute | solution.py:407
  97.2 12.4 %collective-permute-start.21 = (bf16[128,256]{1,0:T(8,128)(2,1)S(1)}, bf16[128,256]{1,0:T(8,128)(2,1)S(1)}, u32[]{:S(2)}, u32[]{:S(2)}) collective-permute-start(bf16[128,256]{1,0:T(8,128)(2,1)S(1)} %add_convert_fusion.1), channel_id=1, source_target_pairs={{0,8},{1,25},{2,10},{3,27},{4,12},{5,29},{6,14},{7,31},{8,40},{9,5... | collective-permute-start | bytes 196616 | tf_op jit(solution)/shard_map/ppermute | solution.py:407
  98.3 11.2 %collective-permute-start.20 = (bf16[128,256]{1,0:T(8,128)(2,1)S(1)}, bf16[128,256]{1,0:T(8,128)(2,1)S(1)}, u32[]{:S(2)}, u32[]{:S(2)}) collective-permute-start(bf16[128,256]{1,0:T(8,128)(2,1)S(1)} %add_convert_fusion.1), channel_id=1, source_target_pairs={{0,0},{1,17},{2,2},{3,19},{4,4},{5,21},{6,6},{7,23},{8,32},{9,49},... | collective-permute-start | bytes 196616 | tf_op jit(solution)/shard_map/ppermute | solution.py:407
  99.0 12.2 %collective-permute-start.27 = (bf16[128,256]{1,0:T(8,128)(2,1)S(1)}, bf16[128,256]{1,0:T(8,128)(2,1)S(1)}, u32[]{:S(2)}, u32[]{:S(2)}) collective-permute-start(bf16[128,256]{1,0:T(8,128)(2,1)S(1)} %add_convert_fusion.p0), channel_id=1, source_target_pairs={{0,32},{32,64},{64,96},{96,0},{1,33},{33,65},{65,97},{97,1},{2,34}... | collective-permute-start | bytes 196616 | tf_op jit(solution)/shard_map/ppermute | solution.py:407
  103.4 9.1 %collective-permute-start.26 = (bf16[128,256]{1,0:T(8,128)(2,1)S(1)}, bf16[128,256]{1,0:T(8,128)(2,1)S(1)}, u32[]{:S(2)}, u32[]{:S(2)}) collective-permute-start(bf16[128,256]{1,0:T(8,128)(2,1)S(1)} %add_convert_fusion.p0), channel_id=1, source_target_pairs={{0,64},{32,96},{64,0},{96,32},{1,65},{33,97},{65,1},{97,33},{2,66}... | collective-permute-start | bytes 196616 | tf_op jit(solution)/shard_map/ppermute | solution.py:407
  109.5 4.3 %collective-permute-start.25 = (bf16[128,256]{1,0:T(8,128)(2,1)S(1)}, bf16[128,256]{1,0:T(8,128)(2,1)S(1)}, u32[]{:S(2)}, u32[]{:S(2)}) collective-permute-start(bf16[128,256]{1,0:T(8,128)(2,1)S(1)} %add_convert_fusion.p0), channel_id=1, source_target_pairs={{0,96},{32,0},{64,32},{96,64},{1,97},{33,1},{65,33},{97,65},{2,98}... | collective-permute-start | bytes 196616 | tf_op jit(solution)/shard_map/ppermute | solution.py:407
  109.5 4.3 %collective-permute-start.23 = (bf16[128,256]{1,0:T(8,128)(2,1)S(1)}, bf16[128,256]{1,0:T(8,128)(2,1)S(1)}, u32[]{:S(2)}, u32[]{:S(2)}) collective-permute-start(bf16[128,256]{1,0:T(8,128)(2,1)S(1)} %collective-permute-done.21.d1), channel_id=1, source_target_pairs={{0,1},{1,0},{2,3},{3,2},{4,5},{5,4},{6,7},{7,6},{8,9},{9,8},{10,11... | collective-permute-start | bytes 196616 | tf_op jit(solution)/shard_map/ppermute | solution.py:407
  109.6 4.2 %collective-permute-start.22 = (bf16[128,256]{1,0:T(8,128)(2,1)S(1)}, bf16[128,256]{1,0:T(8,128)(2,1)S(1)}, u32[]{:S(2)}, u32[]{:S(2)}) collective-permute-start(bf16[128,256]{1,0:T(8,128)(2,1)S(1)} %collective-permute-done.20.d0), channel_id=1, source_target_pairs={{0,1},{1,0},{2,3},{3,2},{4,5},{5,4},{6,7},{7,6},{8,9},{9,8},{10,11... | collective-permute-start | bytes 196616 | tf_op jit(solution)/shard_map/ppermute | solution.py:407
  (5 other events, 121.6 us)
where the time goes:
time: 116 us; the launch traced here: 118 us
  Pallas kernels  50.3 us (43%)
  starting transfers between devices  45.9 us (40%)
  waiting for transfers between devices  18.2 us (16%)
  between operations  1.77 us (2%)
  local copies, waits for them, and re-layouts  1.72 us (1%)
    ppermute x28, starting transfers between devices, send(): return lax.ppermute(x, *move)  45.9 us
    pallas_call x3, Pallas kernels, attend(): pl.pallas_call(kernel, out_shape=outs, in_specs=in_specs, out_specs=[VMEM...  37.9 us
    ppermute x28, waiting for transfers between devices, send(): return lax.ppermute(x, *move)  18.2 us
    pallas_call x1, Pallas kernels, project(): pl.pallas_call(project_kernel, out_shape=(out((R, MSG), BF), out((R, MSG)...  7.29 us
    pallas_call x1, Pallas kernels, finish(): pl.pallas_call(finish_kernel, out_shape=(out((R, D), BF), out((1, R, D),...  3.83 us
  transfers between devices with their start and end apart: 28, of which 10 were waited for; matrix products, arithmetic and copies ran while one was open for 1% of the time, Pallas kernels for 33%

commit v1 on v0

--- a/solution.py
+++ b/solution.py
@@ -133,29 +133,26 @@
 LAST_COST = 5 * 10**9
 
 
-def attend_one(q_of, g_of, own, live, kv, key_t, before, acc, own_acc, ret, scores, dprobs):
-    own_t = own[:, :HD].T
+def attend_some(responses, kv, key_t, before, acc, own_acc, scores, dprobs):
     key_row = lax.broadcasted_iota(jnp.int32, (R, R), 0)
     query_col = lax.broadcasted_iota(jnp.int32, (R, R), 1)
-    allowed = (key_row <= query_col) & live
-    allowed = jnp.concatenate([allowed, allowed], axis=1)
     chunks = [(i, CHUNK) for i in range(0, PRE, CHUNK)] + [(PRE, R)]
-
-    def keys_of(start, size):
-        return own[:, :HD] if start == PRE else kv[start : start + size, :HD]
-
-    def values_of(start, size):
-        return own[:, HD:] if start == PRE else kv[start : start + size, HD:]
-
+    pairs = GROUP // 2
+    items = [(r, j) for r in range(len(responses)) for j in range(pairs)]
     state = {}
 
-    def prepare(j):
+    def prepare(i):
+        r, j = items[i]
+        q_of, g_of, own, live, ret = responses[r]
+        if j == 0:
+            allowed = (key_row <= query_col) & live
+            state["own", r] = own, own[:, :HD].T, jnp.concatenate([allowed, allowed], axis=1)
         two_q, two_g = q_of(j), g_of(j)
         nought = jnp.zeros((R, HD), BF)
         q0, q1 = two_q[:, :HD], two_q[:, HD:]
         g0 = jnp.where(live, two_g[:, :HD], nought)
         g1 = jnp.where(live, two_g[:, HD:], nought)
-        state[j] = dict(
+        state[i] = dict(
             q_rows=jnp.concatenate([q0, q1], axis=0),
             g_rows=jnp.concatenate([g0, g1], axis=0),
             q_t=jnp.concatenate([q0.T, q1.T], axis=1),
@@ -166,73 +163,78 @@
             dq_t=jnp.zeros((HD, KVW), F32),
         )
 
-    def step_a(j, start, size):
-        st = state[j]
-        s = jnp.dot(keys_of(start, size), st["q_t"], preferred_element_type=F32)
+    def step_a(i, start, size):
+        st = state[i]
+        own, _, allowed = state["own", items[i][0]]
+        keys = own[:, :HD] if start == PRE else kv[start : start + size, :HD]
+        s = jnp.dot(keys, st["q_t"], preferred_element_type=F32)
         if start == PRE:
             s = jnp.where(allowed, s, -1e30)
-        scores[j % 2, start : start + size, :] = s
+        scores[i % 2, start : start + size, :] = s
         top = jnp.max(s, axis=0, keepdims=True)
         st["peak"] = top if st["peak"] is None else jnp.maximum(st["peak"], top)
 
-    def step_b(j, start, size):
-        st = state[j]
+    def end_a(i):
+        state[i]["shift"] = state[i]["peak"] * (SCALE * LOG2E)
+
+    def step_b(i, start, size):
+        st = state[i]
         rows = slice(start, start + size)
-        e = jnp.exp2(scores[j % 2, rows, :] * (SCALE * LOG2E) - st["shift"])
-        dp = jnp.dot(values_of(start, size), st["g_t"], preferred_element_type=F32)
+        values = state["own", items[i][0]][0][:, HD:] if start == PRE else kv[rows, HD:]
+        e = jnp.exp2(scores[i % 2, rows, :] * (SCALE * LOG2E) - st["shift"])
+        dp = jnp.dot(values, st["g_t"], preferred_element_type=F32)
         st["total"] += jnp.sum(e, axis=0, keepdims=True)
         st["delta"] += jnp.sum(e * dp, axis=0, keepdims=True)
-        scores[j % 2, rows, :] = e
-        dprobs[j % 2, rows, :] = dp
-
-    def step_c(j, start, size):
-        st = state[j]
+        scores[i % 2, rows, :] = e
+        dprobs[i % 2, rows, :] = dp
+
+    def end_b(i):
+        state[i]["inv"] = 1.0 / state[i]["total"]
+        state[i]["delta"] = state[i]["delta"] * state[i]["inv"]
+
+    def step_c(i, start, size):
+        st = state[i]
+        r, j = items[i]
         rows = slice(start, start + size)
-        p = scores[j % 2, rows, :] * st["inv"]
-        ds = (p * (dprobs[j % 2, rows, :] - st["delta"])).astype(BF)
+        p = scores[i % 2, rows, :] * st["inv"]
+        ds = (p * (dprobs[i % 2, rows, :] - st["delta"])).astype(BF)
         dk = jnp.dot(ds, st["q_rows"], preferred_element_type=F32)
         dv = jnp.dot(p.astype(BF), st["g_rows"], preferred_element_type=F32)
         if start == PRE:
             where, old = own_acc, own_acc if j else None
             rows = slice(0, R)
-            left = own_t
+            left = state["own", r][1]
         else:
-            where, old = acc, acc if j else before
+            where, old = acc, acc if i else before
             left = key_t[:, rows]
         where[rows, :HD] = dk if old is None else old[rows, :HD] + dk
         where[rows, HD:] = dv if old is None else old[rows, HD:] + dv
         st["dq_t"] += jnp.dot(left, ds, preferred_element_type=F32)
 
-    def end_a(j):
-        state[j]["shift"] = state[j]["peak"] * (SCALE * LOG2E)
-
-    def end_b(j):
-        state[j]["inv"] = 1.0 / state[j]["total"]
-        state[j]["delta"] = state[j]["delta"] * state[j]["inv"]
-
-    def end_c(j):
-        dq_t = state[j]["dq_t"] * SCALE
+    def end_c(i):
+        r, j = items[i]
+        ret = responses[r][4]
+        dq_t = state[i]["dq_t"] * SCALE
         ret[:, j * KVW : (j + 1) * KVW] = jnp.concatenate([dq_t[:, :HD].T, dq_t[:, HD:].T], axis=1).astype(BF)
-
-    last = GROUP // 2 - 1
-    prepare(0)
-    for c in chunks:
-        step_a(0, *c)
-    end_a(0)
-    for j in range(GROUP // 2):
-        if j < last:
-            prepare(j + 1)
+        if j == pairs - 1:
+            ret[:, WIDE:] = scaled(own_acc[...])
+
+    n = len(items)
+    for i in range(-1, n):
+        if i + 1 < n:
+            prepare(i + 1)
         for c in chunks:
-            step_b(j, *c)
-            if j < last:
-                step_a(j + 1, *c)
-        end_b(j)
-        if j < last:
-            end_a(j + 1)
-        for c in chunks:
-            step_c(j, *c)
-        end_c(j)
-    ret[:, WIDE:] = scaled(own_acc[...])
+            if i >= 0:
+                step_b(i, *c)
+            if i + 1 < n:
+                step_a(i + 1, *c)
+        if i + 1 < n:
+            end_a(i + 1)
+        if i >= 0:
+            end_b(i)
+            for c in chunks:
+                step_c(i, *c)
+            end_c(i)
 
 
 def scaled(block):
@@ -240,15 +242,14 @@
     return (block * jnp.where(col < HD, SCALE, 1.0)).astype(BF)
 
 
-def attend_bundle(msg, *rest):
+def bundled(msg, ret):
     def q_of(j):
         return msg[:, j * KVW : (j + 1) * KVW]
 
     def g_of(j):
         return msg[:, WIDE + j * KVW : WIDE + (j + 1) * KVW]
 
-    own = msg[:, 2 * WIDE : 2 * WIDE + KVW]
-    attend_one(q_of, g_of, own, msg[:, MSG - HD :] > 0, *rest)
+    return q_of, g_of, msg[:, 2 * WIDE : 2 * WIDE + KVW], msg[:, MSG - HD :] > 0, ret
 
 
 def attend_first_kernel(
@@ -272,16 +273,42 @@
     thin = pl.ds(pl.multiple_of(head * HD, 128), HD)
     own = jnp.concatenate([rk[0, :, thin], rv[0, :, thin]], axis=1)
     live = live_block(length[0]) > 0
-    attend_one(q_of, g_of, own, live, kv, key_t, None, acc, own_acc, ret, scores, dprobs)
-
-
-def attend_mid_kernel(msg_m, msg_p, kv, key_t, before, ret_m, ret_p, acc, own_acc, scores, dprobs):
-    attend_bundle(msg_m, kv, key_t, before, acc, own_acc, ret_m, scores, dprobs)
-    attend_bundle(msg_p, kv, key_t, acc, acc, own_acc, ret_p, scores, dprobs)
+    attend_some([(q_of, g_of, own, live, ret)], kv, key_t, None, acc, own_acc, scores, dprobs)
+
+
+def attend_mid_kernel(msg_m, msg_p, kv, key_t, before, ret_m, ret_p, acc, ret, own_acc, scores, dprobs):
+    acc[...] = before[...]
+
+    def response(r, carry):
+        def either(start, size):
+            cols = slice(start, start + size)
+            return jnp.where(r == 0, msg_m[:, cols], msg_p[:, cols])
+
+        def q_of(j):
+            return either(j * KVW, KVW)
+
+        def g_of(j):
+            return either(WIDE + j * KVW, KVW)
+
+        live = either(MSG - HD, HD) > 0
+        one = q_of, g_of, either(2 * WIDE, KVW), live, ret
+        attend_some([one], kv, key_t, acc, acc, own_acc, scores, dprobs)
+
+        @pl.when(r == 0)
+        def _():
+            ret_m[...] = ret[...]
+
+        @pl.when(r == 1)
+        def _():
+            ret_p[...] = ret[...]
+
+        return carry
+
+    lax.fori_loop(0, 2, response, 0)
 
 
 def attend_last_kernel(msg_2, kv, key_t, before, ret_2, m0, m1, m2, m3, acc, own_acc, scores, dprobs):
-    attend_bundle(msg_2, kv, key_t, before, acc, own_acc, ret_2, scores, dprobs)
+    attend_some([bundled(msg_2, ret_2)], kv, key_t, before, acc, own_acc, scores, dprobs)
     y, z = lax.axis_index("doc"), lax.axis_index("resp") // 2
     for k, out in enumerate((m0, m1, m2, m3)):
         rows = pl.ds(pl.multiple_of(lax.rem(z + k - y + 4, 4) * R, R), R)
@@ -318,7 +345,8 @@
 
 def attend_mid(msg_m, msg_p, kv, key_t, acc):
     outs = [RET_SHAPE, RET_SHAPE, ACC_SHAPE]
-    return attend(attend_mid_kernel, "attend_mid", MID_COST, [VMEM] * 5, outs, [], msg_m, msg_p, kv, key_t, acc)
+    scratch = [pltpu.VMEM((R, RET), BF)]
+    return attend(attend_mid_kernel, "attend_mid", MID_COST, [VMEM] * 5, outs, scratch, msg_m, msg_p, kv, key_t, acc)
 
 
 def attend_last(msg_2, kv, key_t, acc):

time: 116 us -> 105 us (0.905); the launches traced: 118 us -> 105 us
  Pallas kernels: 50.3 us -> 36.9 us
    pallas_call x3, Pallas kernels: 37.9 us -> 24.6 us  [attend(): pl.pallas_call(kernel, out_shape=outs, in_specs=in_specs, out_specs=[VMEM...]
  transfers between devices with their start and end apart: 28 -> 28, of which waited for: 10 -> 10; matrix products, arithmetic and copies ran while one was open for 1% -> 1% of each run, Pallas kernels for 33% -> 25%
where the time goes in v1:
time: 105 us
  starting transfers between devices  45.6 us (43%)
  Pallas kernels  36.9 us (35%)
  waiting for transfers between devices  18.4 us (18%)
  local copies, waits for them, and re-layouts  1.72 us (2%)
  between operations  1.72 us (2%)
    ppermute x28, starting transfers between devices, send(): return lax.ppermute(x, *move)  45.6 us
    pallas_call x3, Pallas kernels, attend(): pl.pallas_call(kernel, out_shape=outs, in_specs=in_specs, out_specs=[VMEM...  24.6 us
    ppermute x28, waiting for transfers between devices, send(): return lax.ppermute(x, *move)  18.4 us
    pallas_call x1, Pallas kernels, project(): pl.pallas_call(project_kernel, out_shape=(out((R, MSG), BF), out((R, MSG)...  7.29 us
    pallas_call x1, Pallas kernels, finish(): pl.pallas_call(finish_kernel, out_shape=(out((R, D), BF), out((1, R, D),...  3.83 us
  transfers between devices with their start and end apart: 28, of which 10 were waited for; matrix products, arithmetic and copies ran while one was open for 1% of the time, Pallas kernels for 25%

profile of v1, /device:TPU:0, one launch (start us, length us, event | category | flops | bytes accessed | tf_op | source)
XLA Modules:
  0.0 104.5 jit_solution(15340279713167872317)
XLA Ops:
  1.3 7.3 %project.1 = (bf16[128,2432]{1,0:T(8,128)(2,1)}, bf16[128,2432]{1,0:T(8,128)(2,1)}, bf16[128,2432]{1,0:T(8,128)(2,1)}, bf16[128,256]{1,0:T(8,128)(2,1)}, bf16[12...) custom-call(s32[1]{0:T(128)S(6)} %copy.15.length, bf16[128,5120]{1,0:T(8,128)(2,1)} %xd.1, ...), custom_call_target="tpu_custom_call" | custom-call | flops 2684354560 | bytes 18874368 | tf_op jit(solution)/shard_map/project/pallas_call | solution.py:101
  8.6 1.7 %collective-permute-start = (bf16[128,256]{1,0:T(8,128)(2,1)}, bf16[128,256]{1,0:T(8,128)(2,1)S(1)}, u32[]{:S(2)}, u32[]{:S(2)}) collective-permute-start(bf16[128,256]{1,0:T(8,128)(2,1)} %get-tuple-element.43), channel_id=1, source_target_pairs={{0,32},{1,97},{2,34},{3,99},{32,64},{33,1},{34,66},{35,3},{64,96},... | collective-permute-start | bytes 196616 | tf_op jit(solution)/shard_map/ppermute | solution.py:435
  10.4 2.9 %collective-permute-start.3 = (bf16[128,256]{1,0:T(8,128)(2,1)}, bf16[128,256]{1,0:T(8,128)(2,1)S(1)}, u32[]{:S(2)}, u32[]{:S(2)}) collective-permute-start(bf16[128,256]{1,0:T(8,128)(2,1)} %get-tuple-element.45), channel_id=1, source_target_pairs={{0,64},{32,96},{64,0},{96,32},{1,65},{33,97},{65,1},{97,33},{2,66}... | collective-permute-start | bytes 196616 | tf_op jit(solution)/shard_map/ppermute | solution.py:435
  13.3 3.0 %collective-permute-start.2 = (bf16[128,256]{1,0:T(8,128)(2,1)}, bf16[128,256]{1,0:T(8,128)(2,1)S(1)}, u32[]{:S(2)}, u32[]{:S(2)}) collective-permute-start(bf16[128,256]{1,0:T(8,128)(2,1)} %get-tuple-element.44), channel_id=1, source_target_pairs={{0,4},{4,0},{8,12},{12,8},{16,20},{20,16},{24,28},{28,24},{1,5},{5... | collective-permute-start | bytes 196616 | tf_op jit(solution)/shard_map/ppermute | solution.py:435
  16.3 1.3 %collective-permute-start.8 = (bf16[128,2432]{1,0:T(8,128)(2,1)}, bf16[128,2432]{1,0:T(8,128)(2,1)S(1)}, u32[]{:S(2)}, u32[]{:S(2)}) collective-permute-start(bf16[128,2432]{1,0:T(8,128)(2,1)} %get-tuple-element.52), channel_id=1, source_target_pairs={{0,96},{32,0},{64,32},{96,64},{1,97},{33,1},{65,33},{97,65},{2,98}... | collective-permute-start | bytes 1867784 | tf_op jit(solution)/shard_map/ppermute | solution.py:435
  19.3 2.0 %collective-permute-start.6 = (bf16[256,256]{1,0:T(8,128)(2,1)S(1)}, bf16[256,256]{1,0:T(8,128)(2,1)S(1)}, u32[]{:S(2)}, u32[]{:S(2)}) collective-permute-start(bf16[256,256]{1,0:T(8,128)(2,1)S(1)} %constant_dynamic-update-slice_fusion.z0), channel_id=1, source_target_pairs={{0,8},{4,12},{8,16},{12,20},{16,24},{20,28},{24,0},{28,4},{1,9},{5... | collective-permute-start | bytes 393224 | tf_op jit(solution)/shard_map/ppermute | solution.py:435
  21.3 3.6 %collective-permute-start.5 = (bf16[256,256]{1,0:T(8,128)(2,1)S(1)}, bf16[256,256]{1,0:T(8,128)(2,1)S(1)}, u32[]{:S(2)}, u32[]{:S(2)}) collective-permute-start(bf16[256,256]{1,0:T(8,128)(2,1)S(1)} %constant_dynamic-update-slice_fusion.z0), channel_id=1, source_target_pairs={{0,16},{4,20},{8,24},{12,28},{16,0},{20,4},{24,8},{28,12},{1,17},{... | collective-permute-start | bytes 393224 | tf_op jit(solution)/shard_map/ppermute | solution.py:435
  25.9 1.6 %collective-permute-done.6.z3 = bf16[256,256]{1,0:T(8,128)(2,1)S(1)} collective-permute-done((bf16[256,256]{1,0:T(8,128)(2,1)S(1)}, bf16[256,256]{1,0:T(8,128)(2,1)S(1)}, u32[]{:S(2)}, u32[]{:S(2)}) %collective-permute-start.6) | collective-permute-done | bytes 131104 | tf_op jit(solution)/shard_map/ppermute | solution.py:435
  27.5 1.1 %collective-permute-start.7 = (bf16[128,2432]{1,0:T(8,128)(2,1)}, bf16[128,2432]{1,0:T(8,128)(2,1)S(1)}, u32[]{:S(2)}, u32[]{:S(2)}) collective-permute-start(bf16[128,2432]{1,0:T(8,128)(2,1)} %get-tuple-element.49), channel_id=1, source_target_pairs={{0,64},{32,96},{64,0},{96,32},{1,65},{33,97},{65,1},{97,33},{2,66}... | collective-permute-start | bytes 1867784 | tf_op jit(solution)/shard_map/ppermute | solution.py:435
  28.5 2.9 %collective-permute-done.5.z2 = bf16[256,256]{1,0:T(8,128)(2,1)S(1)} collective-permute-done((bf16[256,256]{1,0:T(8,128)(2,1)S(1)}, bf16[256,256]{1,0:T(8,128)(2,1)S(1)}, u32[]{:S(2)}, u32[]{:S(2)}) %collective-permute-start.5) | collective-permute-done | bytes 131104 | tf_op jit(solution)/shard_map/ppermute | solution.py:435
  32.3 6.0 %attend_first.1 = (bf16[128,1280]{1,0:T(8,128)(2,1)S(1)}, bf16[1536,256]{1,0:T(8,128)(2,1)S(1)}, bf16[128,1536]{1,0:T(8,128)(2,1)S(1)}, f32[1536,256]{1,0:T(8,128)S(1)}) custom-call(s32[1]{0:T(128)S(6)} %copy.15.length, bf16[1,128,4096]{2,1,0:T(8,128)(2,1)S(1)} %copy-done, bf16[1,128,4096]{2,1,0:T(8,128)(2,1)S(1)} %copy-done.1, ...), custom_call_target="tpu_custom_call" | custom-call | flops 5000000000 | tf_op jit(solution)/shard_map/attend_first/pallas_call | solution.py:324
  38.3 12.5 %attend_mid.1 = (bf16[128,1280]{1,0:T(8,128)(2,1)S(1)}, bf16[128,1280]{1,0:T(8,128)(2,1)S(1)}, f32[1536,256]{1,0:T(8,128)S(1)}) custom-call(bf16[128,2432]{1,0:T(8,128)(2,1)S(1)} %collective-permute-done.8.msg_m, bf16[128,2432]{1,0:T(8,128)(2,1)S(1)} %collective-permute-done.9.msg_p, bf16[1536,256]{1,0:T(8,128)(2,1)S(1)} %get-tuple-element.50.kv, ...), custom_call_target="tpu_custom_call" | custom-call | flops 10000000000 | tf_op jit(solution)/shard_map/attend_mid/pallas_call | solution.py:324
  50.8 2.6 %collective-permute-start.13 = (bf16[128,1280]{1,0:T(8,128)(2,1)S(1)}, bf16[128,1280]{1,0:T(8,128)(2,1)S(1)}, u32[]{:S(2)}, u32[]{:S(2)}) collective-permute-start(bf16[128,1280]{1,0:T(8,128)(2,1)S(1)} %get-tuple-element.60), channel_id=1, source_target_pairs={{0,96},{32,0},{64,32},{96,64},{1,97},{33,1},{65,33},{97,65},{2,98}... | collective-permute-start | bytes 983048 | tf_op jit(solution)/shard_map/ppermute | solution.py:435
  53.5 6.1 %attend_last.1 = (bf16[128,1280]{1,0:T(8,128)(2,1)S(1)}, bf16[384,256]{1,0:T(8,128)(2,1)S(1)}, bf16[384,256]{1,0:T(8,128)(2,1)S(1)}, bf16[384,256]{1,0:T(8,128)(2,1)S(1)}, bf16[384,256]{1,0:T(8,128)(2,1)S(1)}) custom-call(bf16[128,2432]{1,0:T(8,128)(2,1)S(1)} %collective-permute-done.7.msg_2, bf16[1536,256]{1,0:T(8,128)(2,1)S(1)} %get-tuple-element.50.kv, ...), custom_call_target="tpu_custom_call" | custom-call | flops 5000000000 | tf_op jit(solution)/shard_map/attend_last/pallas_call | solution.py:324
  59.6 1.3 %collective-permute-start.10 = (bf16[384,256]{1,0:T(8,128)(2,1)S(1)}, bf16[384,256]{1,0:T(8,128)(2,1)S(1)}, u32[]{:S(2)}, u32[]{:S(2)}) collective-permute-start(bf16[384,256]{1,0:T(8,128)(2,1)S(1)} %get-tuple-element.57), channel_id=1, source_target_pairs={{0,8},{4,12},{8,16},{12,20},{16,24},{20,28},{24,0},{28,4},{1,9},{5... | collective-permute-start | bytes 589832 | tf_op jit(solution)/shard_map/ppermute | solution.py:435
  60.9 2.4 %collective-permute-start.11 = (bf16[384,256]{1,0:T(8,128)(2,1)S(1)}, bf16[384,256]{1,0:T(8,128)(2,1)S(1)}, u32[]{:S(2)}, u32[]{:S(2)}) collective-permute-start(bf16[384,256]{1,0:T(8,128)(2,1)S(1)} %get-tuple-element.58), channel_id=1, source_target_pairs={{0,16},{4,20},{8,24},{12,28},{16,0},{20,4},{24,8},{28,12},{1,17},{... | collective-permute-start | bytes 589832 | tf_op jit(solution)/shard_map/ppermute | solution.py:435
  63.3 1.3 %collective-permute-start.12 = (bf16[384,256]{1,0:T(8,128)(2,1)S(1)}, bf16[384,256]{1,0:T(8,128)(2,1)S(1)}, u32[]{:S(2)}, u32[]{:S(2)}) collective-permute-start(bf16[384,256]{1,0:T(8,128)(2,1)S(1)} %get-tuple-element.59), channel_id=1, source_target_pairs={{0,24},{4,28},{8,0},{12,4},{16,8},{20,12},{24,16},{28,20},{1,25},{... | collective-permute-start | bytes 589832 | tf_op jit(solution)/shard_map/ppermute | solution.py:435
  64.6 3.1 %collective-permute-done.10.m1 = bf16[384,256]{1,0:T(8,128)(2,1)S(1)} collective-permute-done((bf16[384,256]{1,0:T(8,128)(2,1)S(1)}, bf16[384,256]{1,0:T(8,128)(2,1)S(1)}, u32[]{:S(2)}, u32[]{:S(2)}) %collective-permute-start.10) | collective-permute-done | bytes 196640 | tf_op jit(solution)/shard_map/ppermute | solution.py:435
  67.7 4.3 %collective-permute-done.11.m2 = bf16[384,256]{1,0:T(8,128)(2,1)S(1)} collective-permute-done((bf16[384,256]{1,0:T(8,128)(2,1)S(1)}, bf16[384,256]{1,0:T(8,128)(2,1)S(1)}, u32[]{:S(2)}, u32[]{:S(2)}) %collective-permute-start.11) | collective-permute-done | bytes 196640 | tf_op jit(solution)/shard_map/ppermute | solution.py:435
  72.2 1.6 %collective-permute-start.19 = (bf16[128,1280]{1,0:T(8,128)(2,1)S(1)}, bf16[128,1280]{1,0:T(8,128)(2,1)S(1)}, u32[]{:S(2)}, u32[]{:S(2)}) collective-permute-start(bf16[128,1280]{1,0:T(8,128)(2,1)S(1)} %get-tuple-element.68), channel_id=1, source_target_pairs={{0,64},{32,96},{64,0},{96,32},{1,65},{33,97},{65,1},{97,33},{2,66}... | collective-permute-start | bytes 983048 | tf_op jit(solution)/shard_map/ppermute | solution.py:435
  73.8 1.6 %collective-permute-start.18 = (bf16[128,256]{1,0:T(8,128)(2,1)S(1)}, bf16[128,256]{1,0:T(8,128)(2,1)S(1)}, u32[]{:S(2)}, u32[]{:S(2)}) collective-permute-start(bf16[128,256]{1,0:T(8,128)(2,1)S(1)} %add_convert_fusion.2), channel_id=1, source_target_pairs={{0,6},{1,7},{2,0},{3,1},{4,2},{5,3},{6,4},{7,5},{8,14},{9,15},{10,... | collective-permute-start | bytes 196616 | tf_op jit(solution)/shard_map/ppermute | solution.py:435
  75.5 1.1 %collective-permute-start.17 = (bf16[128,256]{1,0:T(8,128)(2,1)S(1)}, bf16[128,256]{1,0:T(8,128)(2,1)S(1)}, u32[]{:S(2)}, u32[]{:S(2)}) collective-permute-start(bf16[128,256]{1,0:T(8,128)(2,1)S(1)} %add_convert_fusion.2), channel_id=1, source_target_pairs={{0,4},{1,5},{2,6},{3,7},{4,0},{5,1},{6,2},{7,3},{8,12},{9,13},{10,... | collective-permute-start | bytes 196616 | tf_op jit(solution)/shard_map/ppermute | solution.py:435
  77.1 2.9 %collective-permute-start.24 = (bf16[128,256]{1,0:T(8,128)(2,1)S(1)}, bf16[128,256]{1,0:T(8,128)(2,1)S(1)}, u32[]{:S(2)}, u32[]{:S(2)}) collective-permute-start(bf16[128,256]{1,0:T(8,128)(2,1)S(1)} %get-tuple-element.76), channel_id=1, source_target_pairs={{0,4},{4,0},{8,12},{12,8},{16,20},{20,16},{24,28},{28,24},{1,5},{5... | collective-permute-start | bytes 196616 | tf_op jit(solution)/shard_map/ppermute | solution.py:435
  80.1 1.9 %collective-permute-done.17 = bf16[128,256]{1,0:T(8,128)(2,1)S(1)} collective-permute-done((bf16[128,256]{1,0:T(8,128)(2,1)S(1)}, bf16[128,256]{1,0:T(8,128)(2,1)S(1)}, u32[]{:S(2)}, u32[]{:S(2)}) %collective-permute-start.17) | collective-permute-done | bytes 65568 | tf_op jit(solution)/shard_map/ppermute | solution.py:435
  82.0 1.1 %collective-permute-done.16 = bf16[128,256]{1,0:T(8,128)(2,1)S(1)} collective-permute-done((bf16[128,256]{1,0:T(8,128)(2,1)S(1)}, bf16[128,256]{1,0:T(8,128)(2,1)S(1)}, u32[]{:S(2)}, u32[]{:S(2)}) %collective-permute-start.16) | collective-permute-done | bytes 65568 | tf_op jit(solution)/shard_map/ppermute | solution.py:435
  83.8 1.2 %collective-permute-start.21 = (bf16[128,256]{1,0:T(8,128)(2,1)S(1)}, bf16[128,256]{1,0:T(8,128)(2,1)S(1)}, u32[]{:S(2)}, u32[]{:S(2)}) collective-permute-start(bf16[128,256]{1,0:T(8,128)(2,1)S(1)} %add_convert_fusion.1), channel_id=1, source_target_pairs={{0,8},{1,25},{2,10},{3,27},{4,12},{5,29},{6,14},{7,31},{8,40},{9,5... | collective-permute-start | bytes 196616 | tf_op jit(solution)/shard_map/ppermute | solution.py:435
  85.7 4.4 %collective-permute-start.27 = (bf16[128,256]{1,0:T(8,128)(2,1)S(1)}, bf16[128,256]{1,0:T(8,128)(2,1)S(1)}, u32[]{:S(2)}, u32[]{:S(2)}) collective-permute-start(bf16[128,256]{1,0:T(8,128)(2,1)S(1)} %add_convert_fusion.p0), channel_id=1, source_target_pairs={{0,32},{32,64},{64,96},{96,0},{1,33},{33,65},{65,97},{97,1},{2,34}... | collective-permute-start | bytes 196616 | tf_op jit(solution)/shard_map/ppermute | solution.py:435
  90.1 6.1 %collective-permute-start.26 = (bf16[128,256]{1,0:T(8,128)(2,1)S(1)}, bf16[128,256]{1,0:T(8,128)(2,1)S(1)}, u32[]{:S(2)}, u32[]{:S(2)}) collective-permute-start(bf16[128,256]{1,0:T(8,128)(2,1)S(1)} %add_convert_fusion.p0), channel_id=1, source_target_pairs={{0,64},{32,96},{64,0},{96,32},{1,65},{33,97},{65,1},{97,33},{2,66}... | collective-permute-start | bytes 196616 | tf_op jit(solution)/shard_map/ppermute | solution.py:435
  96.7 1.2 %unpack.1 = (bf16[1,128,4096]{2,1,0:T(8,128)(2,1)}, bf16[1,128,512]{2,1,0:T(8,128)(2,1)}, bf16[1,128,512]{2,1,0:T(8,128)(2,1)}) custom-call(bf16[128,1280]{1,0:T(8,128)(2,1)S(1)} %get-tuple-element.48.r0, bf16[128,1280]{1,0:T(8,128)(2,1)S(1)} %collective-permute-done.13.r1, bf16[128,1280]{1,0:T(8,128)(2,1)S(1)} %collective-permute-done.19.r2, ...), custom_call_target="tpu_custom_call" | custom-call | bytes 4194304 | tf_op jit(solution)/shard_map/unpack/pallas_call | solution.py:369
  97.9 1.3 %collective-permute-done.26.p2 = bf16[128,256]{1,0:T(8,128)(2,1)S(1)} collective-permute-done((bf16[128,256]{1,0:T(8,128)(2,1)S(1)}, bf16[128,256]{1,0:T(8,128)(2,1)S(1)}, u32[]{:S(2)}, u32[]{:S(2)}) %collective-permute-start.26) | collective-permute-done | bytes 65568 | tf_op jit(solution)/shard_map/ppermute | solution.py:435
  99.1 1.3 %collective-permute-done.25.p1 = bf16[128,256]{1,0:T(8,128)(2,1)S(1)} collective-permute-done((bf16[128,256]{1,0:T(8,128)(2,1)S(1)}, bf16[128,256]{1,0:T(8,128)(2,1)S(1)}, u32[]{:S(2)}, u32[]{:S(2)}) %collective-permute-start.25) | collective-permute-done | bytes 65568 | tf_op jit(solution)/shard_map/ppermute | solution.py:435
  100.5 3.8 %finish.1 = (bf16[128,5120]{1,0:T(8,128)(2,1)}, bf16[1,128,5120]{2,1,0:T(8,128)(2,1)}) custom-call(bf16[128,256]{1,0:T(8,128)(2,1)S(1)} %collective-permute-done.20.d0, bf16[128,256]{1,0:T(8,128)(2,1)S(1)} %collective-permute-done.21.d1, bf16[128,256]{1,0:T(8,128)(2,1)S(1)} %collective-permute-done.22.d2, bf16[128,256]{1,0:T(8,128)(2,1)S(1)} %collective-permute-done.23.d3, ...), custom_call_target="tpu_custom_call" | custom-call | flops 2684354560 | bytes 18874368 | tf_op jit(solution)/shard_map/finish/pallas_call | solution.py:408
  (56 shorter events, 6.3 us)
Async XLA Ops:
  8.6 10.6 %collective-permute-start = (bf16[128,256]{1,0:T(8,128)(2,1)}, bf16[128,256]{1,0:T(8,128)(2,1)S(1)}, u32[]{:S(2)}, u32[]{:S(2)}) collective-permute-start(bf16[128,256]{1,0:T(8,128)(2,1)} %get-tuple-element.43), channel_id=1, source_target_pairs={{0,32},{1,97},{2,34},{3,99},{32,64},{33,1},{34,66},{35,3},{64,96},... | collective-permute-start | bytes 196616 | tf_op jit(solution)/shard_map/ppermute | solution.py:435
  10.4 8.8 %collective-permute-start.3 = (bf16[128,256]{1,0:T(8,128)(2,1)}, bf16[128,256]{1,0:T(8,128)(2,1)S(1)}, u32[]{:S(2)}, u32[]{:S(2)}) collective-permute-start(bf16[128,256]{1,0:T(8,128)(2,1)} %get-tuple-element.45), channel_id=1, source_target_pairs={{0,64},{32,96},{64,0},{96,32},{1,65},{33,97},{65,1},{97,33},{2,66}... | collective-permute-start | bytes 196616 | tf_op jit(solution)/shard_map/ppermute | solution.py:435
  13.3 6.0 %collective-permute-start.2 = (bf16[128,256]{1,0:T(8,128)(2,1)}, bf16[128,256]{1,0:T(8,128)(2,1)S(1)}, u32[]{:S(2)}, u32[]{:S(2)}) collective-permute-start(bf16[128,256]{1,0:T(8,128)(2,1)} %get-tuple-element.44), channel_id=1, source_target_pairs={{0,4},{4,0},{8,12},{12,8},{16,20},{20,16},{24,28},{28,24},{1,5},{5... | collective-permute-start | bytes 196616 | tf_op jit(solution)/shard_map/ppermute | solution.py:435
  16.3 22.0 %collective-permute-start.8 = (bf16[128,2432]{1,0:T(8,128)(2,1)}, bf16[128,2432]{1,0:T(8,128)(2,1)S(1)}, u32[]{:S(2)}, u32[]{:S(2)}) collective-permute-start(bf16[128,2432]{1,0:T(8,128)(2,1)} %get-tuple-element.52), channel_id=1, source_target_pairs={{0,96},{32,0},{64,32},{96,64},{1,97},{33,1},{65,33},{97,65},{2,98}... | collective-permute-start | bytes 1867784 | tf_op jit(solution)/shard_map/ppermute | solution.py:435
  17.6 20.7 %collective-permute-start.9 = (bf16[128,2432]{1,0:T(8,128)(2,1)}, bf16[128,2432]{1,0:T(8,128)(2,1)S(1)}, u32[]{:S(2)}, u32[]{:S(2)}) collective-permute-start(bf16[128,2432]{1,0:T(8,128)(2,1)} %get-tuple-element.53), channel_id=1, source_target_pairs={{0,32},{32,64},{64,96},{96,0},{1,33},{33,65},{65,97},{97,1},{2,34}... | collective-permute-start | bytes 1867784 | tf_op jit(solution)/shard_map/ppermute | solution.py:435
  19.2 5.6 %collective-permute-start.1 = (bf16[128,256]{1,0:T(8,128)(2,1)S(1)}, bf16[128,256]{1,0:T(8,128)(2,1)S(1)}, u32[]{:S(2)}, u32[]{:S(2)}) collective-permute-start(bf16[128,256]{1,0:T(8,128)(2,1)S(1)} %collective-permute-done.mine), channel_id=1, source_target_pairs={{0,1},{1,0},{2,3},{3,2},{4,5},{5,4},{6,7},{7,6},{8,9},{9,8},{10,11... | collective-permute-start | bytes 196616 | tf_op jit(solution)/shard_map/ppermute | solution.py:435
  19.3 8.2 %collective-permute-start.6 = (bf16[256,256]{1,0:T(8,128)(2,1)S(1)}, bf16[256,256]{1,0:T(8,128)(2,1)S(1)}, u32[]{:S(2)}, u32[]{:S(2)}) collective-permute-start(bf16[256,256]{1,0:T(8,128)(2,1)S(1)} %constant_dynamic-update-slice_fusion.z0), channel_id=1, source_target_pairs={{0,8},{4,12},{8,16},{12,20},{16,24},{20,28},{24,0},{28,4},{1,9},{5... | collective-permute-start | bytes 393224 | tf_op jit(solution)/shard_map/ppermute | solution.py:435
  21.3 10.2 %collective-permute-start.5 = (bf16[256,256]{1,0:T(8,128)(2,1)S(1)}, bf16[256,256]{1,0:T(8,128)(2,1)S(1)}, u32[]{:S(2)}, u32[]{:S(2)}) collective-permute-start(bf16[256,256]{1,0:T(8,128)(2,1)S(1)} %constant_dynamic-update-slice_fusion.z0), channel_id=1, source_target_pairs={{0,16},{4,20},{8,24},{12,28},{16,0},{20,4},{24,8},{28,12},{1,17},{... | collective-permute-start | bytes 393224 | tf_op jit(solution)/shard_map/ppermute | solution.py:435
  24.9 6.6 %collective-permute-start.4 = (bf16[256,256]{1,0:T(8,128)(2,1)S(1)}, bf16[256,256]{1,0:T(8,128)(2,1)S(1)}, u32[]{:S(2)}, u32[]{:S(2)}) collective-permute-start(bf16[256,256]{1,0:T(8,128)(2,1)S(1)} %constant_dynamic-update-slice_fusion.z0), channel_id=1, source_target_pairs={{0,24},{4,28},{8,0},{12,4},{16,8},{20,12},{24,16},{28,20},{1,25},{... | collective-permute-start | bytes 393224 | tf_op jit(solution)/shard_map/ppermute | solution.py:435
  27.5 26.0 %collective-permute-start.7 = (bf16[128,2432]{1,0:T(8,128)(2,1)}, bf16[128,2432]{1,0:T(8,128)(2,1)S(1)}, u32[]{:S(2)}, u32[]{:S(2)}) collective-permute-start(bf16[128,2432]{1,0:T(8,128)(2,1)} %get-tuple-element.49), channel_id=1, source_target_pairs={{0,64},{32,96},{64,0},{96,32},{1,65},{33,97},{65,1},{97,33},{2,66}... | collective-permute-start | bytes 1867784 | tf_op jit(solution)/shard_map/ppermute | solution.py:435
  50.8 21.2 %collective-permute-start.13 = (bf16[128,1280]{1,0:T(8,128)(2,1)S(1)}, bf16[128,1280]{1,0:T(8,128)(2,1)S(1)}, u32[]{:S(2)}, u32[]{:S(2)}) collective-permute-start(bf16[128,1280]{1,0:T(8,128)(2,1)S(1)} %get-tuple-element.60), channel_id=1, source_target_pairs={{0,96},{32,0},{64,32},{96,64},{1,97},{33,1},{65,33},{97,65},{2,98}... | collective-permute-start | bytes 983048 | tf_op jit(solution)/shard_map/ppermute | solution.py:435
  53.5 18.5 %collective-permute-start.14 = (bf16[128,1280]{1,0:T(8,128)(2,1)S(1)}, bf16[128,1280]{1,0:T(8,128)(2,1)S(1)}, u32[]{:S(2)}, u32[]{:S(2)}) collective-permute-start(bf16[128,1280]{1,0:T(8,128)(2,1)S(1)} %get-tuple-element.61), channel_id=1, source_target_pairs={{0,32},{32,64},{64,96},{96,0},{1,33},{33,65},{65,97},{97,1},{2,34}... | collective-permute-start | bytes 983048 | tf_op jit(solution)/shard_map/ppermute | solution.py:435
  53.5 47.0 %slice-start = ((s8[5242880]{0:T(1024)(128)(4,1)}), s8[4194304]{0:T(1024)(128)(4,1)S(1)}, s32[]{:S(2)}) async-start(s8[5242880]{0:T(1024)(128)(4,1)} %bitcast), calls=%async_computation | async-start | bytes 8388608
  53.5 47.0 %slice-start.2 = ((s8[5242880]{0:T(1024)(128)(4,1)}), s8[4194304]{0:T(1024)(128)(4,1)S(1)}, s32[]{:S(2)}) async-start(s8[5242880]{0:T(1024)(128)(4,1)} %bitcast.2), calls=%async_computation.2 | async-start | bytes 8388608
  53.5 47.0 %slice-start.1 = ((s8[5242880]{0:T(1024)(128)(4,1)}), s8[1048576]{0:T(1024)(128)(4,1)S(1)}, s32[]{:S(2)}) async-start(s8[5242880]{0:T(1024)(128)(4,1)} %bitcast), calls=%async_computation.1 | async-start | bytes 2097152
  53.5 47.0 %slice-start.3 = ((s8[5242880]{0:T(1024)(128)(4,1)}), s8[1048576]{0:T(1024)(128)(4,1)S(1)}, s32[]{:S(2)}) async-start(s8[5242880]{0:T(1024)(128)(4,1)} %bitcast.2), calls=%async_computation.3 | async-start | bytes 2097152
  59.6 8.0 %collective-permute-start.10 = (bf16[384,256]{1,0:T(8,128)(2,1)S(1)}, bf16[384,256]{1,0:T(8,128)(2,1)S(1)}, u32[]{:S(2)}, u32[]{:S(2)}) collective-permute-start(bf16[384,256]{1,0:T(8,128)(2,1)S(1)} %get-tuple-element.57), channel_id=1, source_target_pairs={{0,8},{4,12},{8,16},{12,20},{16,24},{20,28},{24,0},{28,4},{1,9},{5... | collective-permute-start | bytes 589832 | tf_op jit(solution)/shard_map/ppermute | solution.py:435
  60.9 11.1 %collective-permute-start.11 = (bf16[384,256]{1,0:T(8,128)(2,1)S(1)}, bf16[384,256]{1,0:T(8,128)(2,1)S(1)}, u32[]{:S(2)}, u32[]{:S(2)}) collective-permute-start(bf16[384,256]{1,0:T(8,128)(2,1)S(1)} %get-tuple-element.58), channel_id=1, source_target_pairs={{0,16},{4,20},{8,24},{12,28},{16,0},{20,4},{24,8},{28,12},{1,17},{... | collective-permute-start | bytes 589832 | tf_op jit(solution)/shard_map/ppermute | solution.py:435
  63.3 8.7 %collective-permute-start.12 = (bf16[384,256]{1,0:T(8,128)(2,1)S(1)}, bf16[384,256]{1,0:T(8,128)(2,1)S(1)}, u32[]{:S(2)}, u32[]{:S(2)}) collective-permute-start(bf16[384,256]{1,0:T(8,128)(2,1)S(1)} %get-tuple-element.59), channel_id=1, source_target_pairs={{0,24},{4,28},{8,0},{12,4},{16,8},{20,12},{24,16},{28,20},{1,25},{... | collective-permute-start | bytes 589832 | tf_op jit(solution)/shard_map/ppermute | solution.py:435
  72.1 1.7 %collective-permute-start.15 = (bf16[128,256]{1,0:T(8,128)(2,1)S(1)}, bf16[128,256]{1,0:T(8,128)(2,1)S(1)}, u32[]{:S(2)}, u32[]{:S(2)}) collective-permute-start(bf16[128,256]{1,0:T(8,128)(2,1)S(1)} %get-tuple-element.67), channel_id=1, source_target_pairs={{0,1},{1,0},{2,3},{3,2},{4,5},{5,4},{6,7},{7,6},{8,9},{9,8},{10,11... | collective-permute-start | bytes 196616 | tf_op jit(solution)/shard_map/ppermute | solution.py:435
  72.2 11.6 %collective-permute-start.19 = (bf16[128,1280]{1,0:T(8,128)(2,1)S(1)}, bf16[128,1280]{1,0:T(8,128)(2,1)S(1)}, u32[]{:S(2)}, u32[]{:S(2)}) collective-permute-start(bf16[128,1280]{1,0:T(8,128)(2,1)S(1)} %get-tuple-element.68), channel_id=1, source_target_pairs={{0,64},{32,96},{64,0},{96,32},{1,65},{33,97},{65,1},{97,33},{2,66}... | collective-permute-start | bytes 983048 | tf_op jit(solution)/shard_map/ppermute | solution.py:435
  73.8 6.2 %collective-permute-start.18 = (bf16[128,256]{1,0:T(8,128)(2,1)S(1)}, bf16[128,256]{1,0:T(8,128)(2,1)S(1)}, u32[]{:S(2)}, u32[]{:S(2)}) collective-permute-start(bf16[128,256]{1,0:T(8,128)(2,1)S(1)} %add_convert_fusion.2), channel_id=1, source_target_pairs={{0,6},{1,7},{2,0},{3,1},{4,2},{5,3},{6,4},{7,5},{8,14},{9,15},{10,... | collective-permute-start | bytes 196616 | tf_op jit(solution)/shard_map/ppermute | solution.py:435
  75.5 6.5 %collective-permute-start.17 = (bf16[128,256]{1,0:T(8,128)(2,1)S(1)}, bf16[128,256]{1,0:T(8,128)(2,1)S(1)}, u32[]{:S(2)}, u32[]{:S(2)}) collective-permute-start(bf16[128,256]{1,0:T(8,128)(2,1)S(1)} %add_convert_fusion.2), channel_id=1, source_target_pairs={{0,4},{1,5},{2,6},{3,7},{4,0},{5,1},{6,2},{7,3},{8,12},{9,13},{10,... | collective-permute-start | bytes 196616 | tf_op jit(solution)/shard_map/ppermute | solution.py:435
  76.6 6.5 %collective-permute-start.16 = (bf16[128,256]{1,0:T(8,128)(2,1)S(1)}, bf16[128,256]{1,0:T(8,128)(2,1)S(1)}, u32[]{:S(2)}, u32[]{:S(2)}) collective-permute-start(bf16[128,256]{1,0:T(8,128)(2,1)S(1)} %add_convert_fusion.2), channel_id=1, source_target_pairs={{0,2},{1,3},{2,4},{3,5},{4,6},{5,7},{6,0},{7,1},{8,10},{9,11},{10,... | collective-permute-start | bytes 196616 | tf_op jit(solution)/shard_map/ppermute | solution.py:435
  77.1 8.5 %collective-permute-start.24 = (bf16[128,256]{1,0:T(8,128)(2,1)S(1)}, bf16[128,256]{1,0:T(8,128)(2,1)S(1)}, u32[]{:S(2)}, u32[]{:S(2)}) collective-permute-start(bf16[128,256]{1,0:T(8,128)(2,1)S(1)} %get-tuple-element.76), channel_id=1, source_target_pairs={{0,4},{4,0},{8,12},{12,8},{16,20},{20,16},{24,28},{28,24},{1,5},{5... | collective-permute-start | bytes 196616 | tf_op jit(solution)/shard_map/ppermute | solution.py:435
  83.8 12.4 %collective-permute-start.21 = (bf16[128,256]{1,0:T(8,128)(2,1)S(1)}, bf16[128,256]{1,0:T(8,128)(2,1)S(1)}, u32[]{:S(2)}, u32[]{:S(2)}) collective-permute-start(bf16[128,256]{1,0:T(8,128)(2,1)S(1)} %add_convert_fusion.1), channel_id=1, source_target_pairs={{0,8},{1,25},{2,10},{3,27},{4,12},{5,29},{6,14},{7,31},{8,40},{9,5... | collective-permute-start | bytes 196616 | tf_op jit(solution)/shard_map/ppermute | solution.py:435
  85.0 11.2 %collective-permute-start.20 = (bf16[128,256]{1,0:T(8,128)(2,1)S(1)}, bf16[128,256]{1,0:T(8,128)(2,1)S(1)}, u32[]{:S(2)}, u32[]{:S(2)}) collective-permute-start(bf16[128,256]{1,0:T(8,128)(2,1)S(1)} %add_convert_fusion.1), channel_id=1, source_target_pairs={{0,0},{1,17},{2,2},{3,19},{4,4},{5,21},{6,6},{7,23},{8,32},{9,49},... | collective-permute-start | bytes 196616 | tf_op jit(solution)/shard_map/ppermute | solution.py:435
  85.7 12.2 %collective-permute-start.27 = (bf16[128,256]{1,0:T(8,128)(2,1)S(1)}, bf16[128,256]{1,0:T(8,128)(2,1)S(1)}, u32[]{:S(2)}, u32[]{:S(2)}) collective-permute-start(bf16[128,256]{1,0:T(8,128)(2,1)S(1)} %add_convert_fusion.p0), channel_id=1, source_target_pairs={{0,32},{32,64},{64,96},{96,0},{1,33},{33,65},{65,97},{97,1},{2,34}... | collective-permute-start | bytes 196616 | tf_op jit(solution)/shard_map/ppermute | solution.py:435
  90.1 9.1 %collective-permute-start.26 = (bf16[128,256]{1,0:T(8,128)(2,1)S(1)}, bf16[128,256]{1,0:T(8,128)(2,1)S(1)}, u32[]{:S(2)}, u32[]{:S(2)}) collective-permute-start(bf16[128,256]{1,0:T(8,128)(2,1)S(1)} %add_convert_fusion.p0), channel_id=1, source_target_pairs={{0,64},{32,96},{64,0},{96,32},{1,65},{33,97},{65,1},{97,33},{2,66}... | collective-permute-start | bytes 196616 | tf_op jit(solution)/shard_map/ppermute | solution.py:435
  96.2 4.3 %collective-permute-start.25 = (bf16[128,256]{1,0:T(8,128)(2,1)S(1)}, bf16[128,256]{1,0:T(8,128)(2,1)S(1)}, u32[]{:S(2)}, u32[]{:S(2)}) collective-permute-start(bf16[128,256]{1,0:T(8,128)(2,1)S(1)} %add_convert_fusion.p0), channel_id=1, source_target_pairs={{0,96},{32,0},{64,32},{96,64},{1,97},{33,1},{65,33},{97,65},{2,98}... | collective-permute-start | bytes 196616 | tf_op jit(solution)/shard_map/ppermute | solution.py:435
  96.2 4.3 %collective-permute-start.23 = (bf16[128,256]{1,0:T(8,128)(2,1)S(1)}, bf16[128,256]{1,0:T(8,128)(2,1)S(1)}, u32[]{:S(2)}, u32[]{:S(2)}) collective-permute-start(bf16[128,256]{1,0:T(8,128)(2,1)S(1)} %collective-permute-done.21.d1), channel_id=1, source_target_pairs={{0,1},{1,0},{2,3},{3,2},{4,5},{5,4},{6,7},{7,6},{8,9},{9,8},{10,11... | collective-permute-start | bytes 196616 | tf_op jit(solution)/shard_map/ppermute | solution.py:435
  96.2 4.2 %collective-permute-start.22 = (bf16[128,256]{1,0:T(8,128)(2,1)S(1)}, bf16[128,256]{1,0:T(8,128)(2,1)S(1)}, u32[]{:S(2)}, u32[]{:S(2)}) collective-permute-start(bf16[128,256]{1,0:T(8,128)(2,1)S(1)} %collective-permute-done.20.d0), channel_id=1, source_target_pairs={{0,1},{1,0},{2,3},{3,2},{4,5},{5,4},{6,7},{7,6},{8,9},{9,8},{10,11... | collective-permute-start | bytes 196616 | tf_op jit(solution)/shard_map/ppermute | solution.py:435
  (5 other events, 121.6 us)

commit v2 on v1

--- a/solution.py
+++ b/solution.py
@@ -530,7 +530,7 @@
     doc = added(doc, send(doc, other_core())).astype(BF)
     doc = added(doc, *(send(doc, along_x(k)) for k in (1, 2, 3))).astype(BF)
     prompt = added(keep, send(give, other_half())).astype(BF)
-    doc, ret_2 = lax.optimization_barrier((doc, ret_2))
+    prompt, ret_2 = lax.optimization_barrier((prompt, ret_2))
     mine = [send(doc, cross(0, 2)), send(doc, cross(1, 3))]
     docs = mine + [send(piece, other_core()) for piece in mine]
     prompts = [prompt] + [send(prompt, along_y(-k)) for k in (1, 2, 3)]

time: 105 us -> 104 us (level)
  starting transfers between devices: 45.6 us -> 41.9 us
  waiting for transfers between devices: 18.4 us -> 21.1 us
    ppermute x28, starting transfers between devices: 45.6 us -> 41.9 us  [send(): return lax.ppermute(x, *move)]
    ppermute x28, waiting for transfers between devices: 18.4 us -> 21.1 us  [send(): return lax.ppermute(x, *move)]
  transfers between devices with their start and end apart: 28 -> 28, of which waited for: 10 -> 11; matrix products, arithmetic and copies ran while one was open for 1% -> 1% of each run, Pallas kernels for 25% -> 25%
where the time goes in v2:
time: 104 us; the launch traced here: 103 us
  starting transfers between devices  41.9 us (40%)
  Pallas kernels  36.9 us (35%)
  waiting for transfers between devices  21.1 us (20%)
  local copies, waits for them, and re-layouts  1.72 us (2%)
  between operations  1.72 us (2%)
    ppermute x28, starting transfers between devices, send(): return lax.ppermute(x, *move)  41.9 us
    pallas_call x3, Pallas kernels, attend(): pl.pallas_call(kernel, out_shape=outs, in_specs=in_specs, out_specs=[VMEM...  24.6 us
    ppermute x28, waiting for transfers between devices, send(): return lax.ppermute(x, *move)  21.1 us
    pallas_call x1, Pallas kernels, project(): pl.pallas_call(project_kernel, out_shape=(out((R, MSG), BF), out((R, MSG)...  7.29 us
    pallas_call x1, Pallas kernels, finish(): pl.pallas_call(finish_kernel, out_shape=(out((R, D), BF), out((1, R, D),...  3.83 us
  transfers between devices with their start and end apart: 28, of which 11 were waited for; matrix products, arithmetic and copies ran while one was open for 1% of the time, Pallas kernels for 25%

profile of v2, /device:TPU:0, one launch (start us, length us, event | category | flops | bytes accessed | tf_op | source)
XLA Modules:
  0.0 103.5 jit_solution(16281502884813908209)
XLA Ops:
  1.3 7.3 %project.1 = (bf16[128,2432]{1,0:T(8,128)(2,1)}, bf16[128,2432]{1,0:T(8,128)(2,1)}, bf16[128,2432]{1,0:T(8,128)(2,1)}, bf16[128,256]{1,0:T(8,128)(2,1)}, bf16[12...) custom-call(s32[1]{0:T(128)S(6)} %copy.15.length, bf16[128,5120]{1,0:T(8,128)(2,1)} %xd.1, ...), custom_call_target="tpu_custom_call" | custom-call | flops 2684354560 | bytes 18874368 | tf_op jit(solution)/shard_map/project/pallas_call | solution.py:101
  8.6 1.7 %collective-permute-start = (bf16[128,256]{1,0:T(8,128)(2,1)}, bf16[128,256]{1,0:T(8,128)(2,1)S(1)}, u32[]{:S(2)}, u32[]{:S(2)}) collective-permute-start(bf16[128,256]{1,0:T(8,128)(2,1)} %get-tuple-element.43), channel_id=1, source_target_pairs={{0,32},{1,97},{2,34},{3,99},{32,64},{33,1},{34,66},{35,3},{64,96},... | collective-permute-start | bytes 196616 | tf_op jit(solution)/shard_map/ppermute | solution.py:435
  10.4 2.9 %collective-permute-start.3 = (bf16[128,256]{1,0:T(8,128)(2,1)}, bf16[128,256]{1,0:T(8,128)(2,1)S(1)}, u32[]{:S(2)}, u32[]{:S(2)}) collective-permute-start(bf16[128,256]{1,0:T(8,128)(2,1)} %get-tuple-element.45), channel_id=1, source_target_pairs={{0,64},{32,96},{64,0},{96,32},{1,65},{33,97},{65,1},{97,33},{2,66}... | collective-permute-start | bytes 196616 | tf_op jit(solution)/shard_map/ppermute | solution.py:435
  13.3 3.0 %collective-permute-start.2 = (bf16[128,256]{1,0:T(8,128)(2,1)}, bf16[128,256]{1,0:T(8,128)(2,1)S(1)}, u32[]{:S(2)}, u32[]{:S(2)}) collective-permute-start(bf16[128,256]{1,0:T(8,128)(2,1)} %get-tuple-element.44), channel_id=1, source_target_pairs={{0,4},{4,0},{8,12},{12,8},{16,20},{20,16},{24,28},{28,24},{1,5},{5... | collective-permute-start | bytes 196616 | tf_op jit(solution)/shard_map/ppermute | solution.py:435
  16.3 1.3 %collective-permute-start.8 = (bf16[128,2432]{1,0:T(8,128)(2,1)}, bf16[128,2432]{1,0:T(8,128)(2,1)S(1)}, u32[]{:S(2)}, u32[]{:S(2)}) collective-permute-start(bf16[128,2432]{1,0:T(8,128)(2,1)} %get-tuple-element.52), channel_id=1, source_target_pairs={{0,96},{32,0},{64,32},{96,64},{1,97},{33,1},{65,33},{97,65},{2,98}... | collective-permute-start | bytes 1867784 | tf_op jit(solution)/shard_map/ppermute | solution.py:435
  19.3 2.0 %collective-permute-start.6 = (bf16[256,256]{1,0:T(8,128)(2,1)S(1)}, bf16[256,256]{1,0:T(8,128)(2,1)S(1)}, u32[]{:S(2)}, u32[]{:S(2)}) collective-permute-start(bf16[256,256]{1,0:T(8,128)(2,1)S(1)} %constant_dynamic-update-slice_fusion.z0), channel_id=1, source_target_pairs={{0,8},{4,12},{8,16},{12,20},{16,24},{20,28},{24,0},{28,4},{1,9},{5... | collective-permute-start | bytes 393224 | tf_op jit(solution)/shard_map/ppermute | solution.py:435
  21.3 3.6 %collective-permute-start.5 = (bf16[256,256]{1,0:T(8,128)(2,1)S(1)}, bf16[256,256]{1,0:T(8,128)(2,1)S(1)}, u32[]{:S(2)}, u32[]{:S(2)}) collective-permute-start(bf16[256,256]{1,0:T(8,128)(2,1)S(1)} %constant_dynamic-update-slice_fusion.z0), channel_id=1, source_target_pairs={{0,16},{4,20},{8,24},{12,28},{16,0},{20,4},{24,8},{28,12},{1,17},{... | collective-permute-start | bytes 393224 | tf_op jit(solution)/shard_map/ppermute | solution.py:435
  24.9 1.0 collective-permute-start.4
  25.9 1.6 %collective-permute-done.6.z3 = bf16[256,256]{1,0:T(8,128)(2,1)S(1)} collective-permute-done((bf16[256,256]{1,0:T(8,128)(2,1)S(1)}, bf16[256,256]{1,0:T(8,128)(2,1)S(1)}, u32[]{:S(2)}, u32[]{:S(2)}) %collective-permute-start.6) | collective-permute-done | bytes 131104 | tf_op jit(solution)/shard_map/ppermute | solution.py:435
  27.5 1.1 %collective-permute-start.7 = (bf16[128,2432]{1,0:T(8,128)(2,1)}, bf16[128,2432]{1,0:T(8,128)(2,1)S(1)}, u32[]{:S(2)}, u32[]{:S(2)}) collective-permute-start(bf16[128,2432]{1,0:T(8,128)(2,1)} %get-tuple-element.49), channel_id=1, source_target_pairs={{0,64},{32,96},{64,0},{96,32},{1,65},{33,97},{65,1},{97,33},{2,66}... | collective-permute-start | bytes 1867784 | tf_op jit(solution)/shard_map/ppermute | solution.py:435
  28.5 2.9 %collective-permute-done.5.z2 = bf16[256,256]{1,0:T(8,128)(2,1)S(1)} collective-permute-done((bf16[256,256]{1,0:T(8,128)(2,1)S(1)}, bf16[256,256]{1,0:T(8,128)(2,1)S(1)}, u32[]{:S(2)}, u32[]{:S(2)}) %collective-permute-start.5) | collective-permute-done | bytes 131104 | tf_op jit(solution)/shard_map/ppermute | solution.py:435
  32.3 6.0 %attend_first.1 = (bf16[128,1280]{1,0:T(8,128)(2,1)S(1)}, bf16[1536,256]{1,0:T(8,128)(2,1)S(1)}, bf16[128,1536]{1,0:T(8,128)(2,1)S(1)}, f32[1536,256]{1,0:T(8,128)S(1)}) custom-call(s32[1]{0:T(128)S(6)} %copy.15.length, bf16[1,128,4096]{2,1,0:T(8,128)(2,1)S(1)} %copy-done, bf16[1,128,4096]{2,1,0:T(8,128)(2,1)S(1)} %copy-done.1, ...), custom_call_target="tpu_custom_call" | custom-call | flops 5000000000 | tf_op jit(solution)/shard_map/attend_first/pallas_call | solution.py:324
  38.3 12.5 %attend_mid.1 = (bf16[128,1280]{1,0:T(8,128)(2,1)S(1)}, bf16[128,1280]{1,0:T(8,128)(2,1)S(1)}, f32[1536,256]{1,0:T(8,128)S(1)}) custom-call(bf16[128,2432]{1,0:T(8,128)(2,1)S(1)} %collective-permute-done.8.msg_m, bf16[128,2432]{1,0:T(8,128)(2,1)S(1)} %collective-permute-done.9.msg_p, bf16[1536,256]{1,0:T(8,128)(2,1)S(1)} %get-tuple-element.50.kv, ...), custom_call_target="tpu_custom_call" | custom-call | flops 10000000000 | tf_op jit(solution)/shard_map/attend_mid/pallas_call | solution.py:324
  50.8 2.6 %collective-permute-start.13 = (bf16[128,1280]{1,0:T(8,128)(2,1)S(1)}, bf16[128,1280]{1,0:T(8,128)(2,1)S(1)}, u32[]{:S(2)}, u32[]{:S(2)}) collective-permute-start(bf16[128,1280]{1,0:T(8,128)(2,1)S(1)} %get-tuple-element.60), channel_id=1, source_target_pairs={{0,96},{32,0},{64,32},{96,64},{1,97},{33,1},{65,33},{97,65},{2,98}... | collective-permute-start | bytes 983048 | tf_op jit(solution)/shard_map/ppermute | solution.py:435
  53.5 6.1 %attend_last.1 = (bf16[128,1280]{1,0:T(8,128)(2,1)S(1)}, bf16[384,256]{1,0:T(8,128)(2,1)S(1)}, bf16[384,256]{1,0:T(8,128)(2,1)S(1)}, bf16[384,256]{1,0:T(8,128)(2,1)S(1)}, bf16[384,256]{1,0:T(8,128)(2,1)S(1)}) custom-call(bf16[128,2432]{1,0:T(8,128)(2,1)S(1)} %collective-permute-done.7.msg_2, bf16[1536,256]{1,0:T(8,128)(2,1)S(1)} %get-tuple-element.50.kv, ...), custom_call_target="tpu_custom_call" | custom-call | flops 5000000000 | tf_op jit(solution)/shard_map/attend_last/pallas_call | solution.py:324
  59.6 1.3 %collective-permute-start.10 = (bf16[384,256]{1,0:T(8,128)(2,1)S(1)}, bf16[384,256]{1,0:T(8,128)(2,1)S(1)}, u32[]{:S(2)}, u32[]{:S(2)}) collective-permute-start(bf16[384,256]{1,0:T(8,128)(2,1)S(1)} %get-tuple-element.57), channel_id=1, source_target_pairs={{0,8},{4,12},{8,16},{12,20},{16,24},{20,28},{24,0},{28,4},{1,9},{5... | collective-permute-start | bytes 589832 | tf_op jit(solution)/shard_map/ppermute | solution.py:435
  60.9 2.4 %collective-permute-start.11 = (bf16[384,256]{1,0:T(8,128)(2,1)S(1)}, bf16[384,256]{1,0:T(8,128)(2,1)S(1)}, u32[]{:S(2)}, u32[]{:S(2)}) collective-permute-start(bf16[384,256]{1,0:T(8,128)(2,1)S(1)} %get-tuple-element.58), channel_id=1, source_target_pairs={{0,16},{4,20},{8,24},{12,28},{16,0},{20,4},{24,8},{28,12},{1,17},{... | collective-permute-start | bytes 589832 | tf_op jit(solution)/shard_map/ppermute | solution.py:435
  63.3 1.3 %collective-permute-start.12 = (bf16[384,256]{1,0:T(8,128)(2,1)S(1)}, bf16[384,256]{1,0:T(8,128)(2,1)S(1)}, u32[]{:S(2)}, u32[]{:S(2)}) collective-permute-start(bf16[384,256]{1,0:T(8,128)(2,1)S(1)} %get-tuple-element.59), channel_id=1, source_target_pairs={{0,24},{4,28},{8,0},{12,4},{16,8},{20,12},{24,16},{28,20},{1,25},{... | collective-permute-start | bytes 589832 | tf_op jit(solution)/shard_map/ppermute | solution.py:435
  64.6 3.1 %collective-permute-done.10.m1 = bf16[384,256]{1,0:T(8,128)(2,1)S(1)} collective-permute-done((bf16[384,256]{1,0:T(8,128)(2,1)S(1)}, bf16[384,256]{1,0:T(8,128)(2,1)S(1)}, u32[]{:S(2)}, u32[]{:S(2)}) %collective-permute-start.10) | collective-permute-done | bytes 196640 | tf_op jit(solution)/shard_map/ppermute | solution.py:435
  67.7 4.3 %collective-permute-done.11.m2 = bf16[384,256]{1,0:T(8,128)(2,1)S(1)} collective-permute-done((bf16[384,256]{1,0:T(8,128)(2,1)S(1)}, bf16[384,256]{1,0:T(8,128)(2,1)S(1)}, u32[]{:S(2)}, u32[]{:S(2)}) %collective-permute-start.11) | collective-permute-done | bytes 196640 | tf_op jit(solution)/shard_map/ppermute | solution.py:435
  72.2 1.2 %collective-permute-done.17 = bf16[128,256]{1,0:T(8,128)(2,1)S(1)} collective-permute-done((bf16[128,256]{1,0:T(8,128)(2,1)S(1)}, bf16[128,256]{1,0:T(8,128)(2,1)S(1)}, u32[]{:S(2)}, u32[]{:S(2)}) %collective-permute-start.17) | collective-permute-done | bytes 65568 | tf_op jit(solution)/shard_map/ppermute | solution.py:435
  73.5 2.0 %collective-permute-start.20 = (bf16[128,256]{1,0:T(8,128)(2,1)S(1)}, bf16[128,256]{1,0:T(8,128)(2,1)S(1)}, u32[]{:S(2)}, u32[]{:S(2)}) collective-permute-start(bf16[128,256]{1,0:T(8,128)(2,1)S(1)} %add_convert_fusion.1), channel_id=1, source_target_pairs={{0,6},{1,7},{2,0},{3,1},{4,2},{5,3},{6,4},{7,5},{8,14},{9,15},{10,... | collective-permute-start | bytes 196616 | tf_op jit(solution)/shard_map/ppermute | solution.py:435
  77.1 1.2 %collective-permute-start.16 = (bf16[128,1280]{1,0:T(8,128)(2,1)S(1)}, bf16[128,1280]{1,0:T(8,128)(2,1)S(1)}, u32[]{:S(2)}, u32[]{:S(2)}) collective-permute-start(bf16[128,1280]{1,0:T(8,128)(2,1)S(1)} %get-tuple-element.69), channel_id=1, source_target_pairs={{0,64},{32,96},{64,0},{96,32},{1,65},{33,97},{65,1},{97,33},{2,66}... | collective-permute-start | bytes 983048 | tf_op jit(solution)/shard_map/ppermute | solution.py:435
  78.3 2.9 %collective-permute-start.15 = (bf16[128,256]{1,0:T(8,128)(2,1)S(1)}, bf16[128,256]{1,0:T(8,128)(2,1)S(1)}, u32[]{:S(2)}, u32[]{:S(2)}) collective-permute-start(bf16[128,256]{1,0:T(8,128)(2,1)S(1)} %get-tuple-element.68), channel_id=1, source_target_pairs={{0,4},{4,0},{8,12},{12,8},{16,20},{20,16},{24,28},{28,24},{1,5},{5... | collective-permute-start | bytes 196616 | tf_op jit(solution)/shard_map/ppermute | solution.py:435
  81.7 1.2 %collective-permute-done.18 = bf16[128,256]{1,0:T(8,128)(2,1)S(1)} collective-permute-done((bf16[128,256]{1,0:T(8,128)(2,1)S(1)}, bf16[128,256]{1,0:T(8,128)(2,1)S(1)}, u32[]{:S(2)}, u32[]{:S(2)}) %collective-permute-start.18) | collective-permute-done | bytes 65568 | tf_op jit(solution)/shard_map/ppermute | solution.py:435
  83.0 1.2 %collective-permute-start.22 = (bf16[128,256]{1,0:T(8,128)(2,1)S(1)}, bf16[128,256]{1,0:T(8,128)(2,1)S(1)}, u32[]{:S(2)}, u32[]{:S(2)}) collective-permute-start(bf16[128,256]{1,0:T(8,128)(2,1)S(1)} %add_convert_fusion), channel_id=1, source_target_pairs={{0,8},{1,25},{2,10},{3,27},{4,12},{5,29},{6,14},{7,31},{8,40},{9,5... | collective-permute-start | bytes 196616 | tf_op jit(solution)/shard_map/ppermute | solution.py:435
  84.9 3.5 %collective-permute-done.16.r2 = bf16[128,1280]{1,0:T(8,128)(2,1)S(1)} collective-permute-done((bf16[128,1280]{1,0:T(8,128)(2,1)S(1)}, bf16[128,1280]{1,0:T(8,128)(2,1)S(1)}, u32[]{:S(2)}, u32[]{:S(2)}) %collective-permute-start.16) | collective-permute-done | bytes 327712 | tf_op jit(solution)/shard_map/ppermute | solution.py:435
  88.4 6.8 %collective-permute-start.26 = (bf16[128,256]{1,0:T(8,128)(2,1)S(1)}, bf16[128,256]{1,0:T(8,128)(2,1)S(1)}, u32[]{:S(2)}, u32[]{:S(2)}) collective-permute-start(bf16[128,256]{1,0:T(8,128)(2,1)S(1)} %add_convert_fusion.2.p0), channel_id=1, source_target_pairs={{0,64},{32,96},{64,0},{96,32},{1,65},{33,97},{65,1},{97,33},{2,66}... | collective-permute-start | bytes 196616 | tf_op jit(solution)/shard_map/ppermute | solution.py:435
  95.7 1.2 %unpack.1 = (bf16[1,128,4096]{2,1,0:T(8,128)(2,1)}, bf16[1,128,512]{2,1,0:T(8,128)(2,1)}, bf16[1,128,512]{2,1,0:T(8,128)(2,1)}) custom-call(bf16[128,1280]{1,0:T(8,128)(2,1)S(1)} %get-tuple-element.48.r0, bf16[128,1280]{1,0:T(8,128)(2,1)S(1)} %collective-permute-done.13.r1, bf16[128,1280]{1,0:T(8,128)(2,1)S(1)} %collective-permute-done.16.r2, ...), custom_call_target="tpu_custom_call" | custom-call | bytes 4194304 | tf_op jit(solution)/shard_map/unpack/pallas_call | solution.py:369
  96.8 1.3 %collective-permute-done.26.p2 = bf16[128,256]{1,0:T(8,128)(2,1)S(1)} collective-permute-done((bf16[128,256]{1,0:T(8,128)(2,1)S(1)}, bf16[128,256]{1,0:T(8,128)(2,1)S(1)}, u32[]{:S(2)}, u32[]{:S(2)}) %collective-permute-start.26) | collective-permute-done | bytes 65568 | tf_op jit(solution)/shard_map/ppermute | solution.py:435
  98.1 1.3 %collective-permute-done.25.p1 = bf16[128,256]{1,0:T(8,128)(2,1)S(1)} collective-permute-done((bf16[128,256]{1,0:T(8,128)(2,1)S(1)}, bf16[128,256]{1,0:T(8,128)(2,1)S(1)}, u32[]{:S(2)}, u32[]{:S(2)}) %collective-permute-start.25) | collective-permute-done | bytes 65568 | tf_op jit(solution)/shard_map/ppermute | solution.py:435
  99.5 3.8 %finish.1 = (bf16[128,5120]{1,0:T(8,128)(2,1)}, bf16[1,128,5120]{2,1,0:T(8,128)(2,1)}) custom-call(bf16[128,256]{1,0:T(8,128)(2,1)S(1)} %collective-permute-done.21.d0, bf16[128,256]{1,0:T(8,128)(2,1)S(1)} %collective-permute-done.22.d1, bf16[128,256]{1,0:T(8,128)(2,1)S(1)} %collective-permute-done.23.d2, bf16[128,256]{1,0:T(8,128)(2,1)S(1)} %collective-permute-done.24.d3, ...), custom_call_target="tpu_custom_call" | custom-call | flops 2684354560 | bytes 18874368 | tf_op jit(solution)/shard_map/finish/pallas_call | solution.py:408
  (56 shorter events, 6.1 us)
Async XLA Ops:
  8.6 10.6 %collective-permute-start = (bf16[128,256]{1,0:T(8,128)(2,1)}, bf16[128,256]{1,0:T(8,128)(2,1)S(1)}, u32[]{:S(2)}, u32[]{:S(2)}) collective-permute-start(bf16[128,256]{1,0:T(8,128)(2,1)} %get-tuple-element.43), channel_id=1, source_target_pairs={{0,32},{1,97},{2,34},{3,99},{32,64},{33,1},{34,66},{35,3},{64,96},... | collective-permute-start | bytes 196616 | tf_op jit(solution)/shard_map/ppermute | solution.py:435
  10.4 8.8 %collective-permute-start.3 = (bf16[128,256]{1,0:T(8,128)(2,1)}, bf16[128,256]{1,0:T(8,128)(2,1)S(1)}, u32[]{:S(2)}, u32[]{:S(2)}) collective-permute-start(bf16[128,256]{1,0:T(8,128)(2,1)} %get-tuple-element.45), channel_id=1, source_target_pairs={{0,64},{32,96},{64,0},{96,32},{1,65},{33,97},{65,1},{97,33},{2,66}... | collective-permute-start | bytes 196616 | tf_op jit(solution)/shard_map/ppermute | solution.py:435
  13.3 6.0 %collective-permute-start.2 = (bf16[128,256]{1,0:T(8,128)(2,1)}, bf16[128,256]{1,0:T(8,128)(2,1)S(1)}, u32[]{:S(2)}, u32[]{:S(2)}) collective-permute-start(bf16[128,256]{1,0:T(8,128)(2,1)} %get-tuple-element.44), channel_id=1, source_target_pairs={{0,4},{4,0},{8,12},{12,8},{16,20},{20,16},{24,28},{28,24},{1,5},{5... | collective-permute-start | bytes 196616 | tf_op jit(solution)/shard_map/ppermute | solution.py:435
  16.3 22.0 %collective-permute-start.8 = (bf16[128,2432]{1,0:T(8,128)(2,1)}, bf16[128,2432]{1,0:T(8,128)(2,1)S(1)}, u32[]{:S(2)}, u32[]{:S(2)}) collective-permute-start(bf16[128,2432]{1,0:T(8,128)(2,1)} %get-tuple-element.52), channel_id=1, source_target_pairs={{0,96},{32,0},{64,32},{96,64},{1,97},{33,1},{65,33},{97,65},{2,98}... | collective-permute-start | bytes 1867784 | tf_op jit(solution)/shard_map/ppermute | solution.py:435
  17.6 20.7 %collective-permute-start.9 = (bf16[128,2432]{1,0:T(8,128)(2,1)}, bf16[128,2432]{1,0:T(8,128)(2,1)S(1)}, u32[]{:S(2)}, u32[]{:S(2)}) collective-permute-start(bf16[128,2432]{1,0:T(8,128)(2,1)} %get-tuple-element.53), channel_id=1, source_target_pairs={{0,32},{32,64},{64,96},{96,0},{1,33},{33,65},{65,97},{97,1},{2,34}... | collective-permute-start | bytes 1867784 | tf_op jit(solution)/shard_map/ppermute | solution.py:435
  19.2 5.6 %collective-permute-start.1 = (bf16[128,256]{1,0:T(8,128)(2,1)S(1)}, bf16[128,256]{1,0:T(8,128)(2,1)S(1)}, u32[]{:S(2)}, u32[]{:S(2)}) collective-permute-start(bf16[128,256]{1,0:T(8,128)(2,1)S(1)} %collective-permute-done.mine), channel_id=1, source_target_pairs={{0,1},{1,0},{2,3},{3,2},{4,5},{5,4},{6,7},{7,6},{8,9},{9,8},{10,11... | collective-permute-start | bytes 196616 | tf_op jit(solution)/shard_map/ppermute | solution.py:435
  19.3 8.2 %collective-permute-start.6 = (bf16[256,256]{1,0:T(8,128)(2,1)S(1)}, bf16[256,256]{1,0:T(8,128)(2,1)S(1)}, u32[]{:S(2)}, u32[]{:S(2)}) collective-permute-start(bf16[256,256]{1,0:T(8,128)(2,1)S(1)} %constant_dynamic-update-slice_fusion.z0), channel_id=1, source_target_pairs={{0,8},{4,12},{8,16},{12,20},{16,24},{20,28},{24,0},{28,4},{1,9},{5... | collective-permute-start | bytes 393224 | tf_op jit(solution)/shard_map/ppermute | solution.py:435
  21.3 10.2 %collective-permute-start.5 = (bf16[256,256]{1,0:T(8,128)(2,1)S(1)}, bf16[256,256]{1,0:T(8,128)(2,1)S(1)}, u32[]{:S(2)}, u32[]{:S(2)}) collective-permute-start(bf16[256,256]{1,0:T(8,128)(2,1)S(1)} %constant_dynamic-update-slice_fusion.z0), channel_id=1, source_target_pairs={{0,16},{4,20},{8,24},{12,28},{16,0},{20,4},{24,8},{28,12},{1,17},{... | collective-permute-start | bytes 393224 | tf_op jit(solution)/shard_map/ppermute | solution.py:435
  24.9 6.6 %collective-permute-start.4 = (bf16[256,256]{1,0:T(8,128)(2,1)S(1)}, bf16[256,256]{1,0:T(8,128)(2,1)S(1)}, u32[]{:S(2)}, u32[]{:S(2)}) collective-permute-start(bf16[256,256]{1,0:T(8,128)(2,1)S(1)} %constant_dynamic-update-slice_fusion.z0), channel_id=1, source_target_pairs={{0,24},{4,28},{8,0},{12,4},{16,8},{20,12},{24,16},{28,20},{1,25},{... | collective-permute-start | bytes 393224 | tf_op jit(solution)/shard_map/ppermute | solution.py:435
  27.5 26.0 %collective-permute-start.7 = (bf16[128,2432]{1,0:T(8,128)(2,1)}, bf16[128,2432]{1,0:T(8,128)(2,1)S(1)}, u32[]{:S(2)}, u32[]{:S(2)}) collective-permute-start(bf16[128,2432]{1,0:T(8,128)(2,1)} %get-tuple-element.49), channel_id=1, source_target_pairs={{0,64},{32,96},{64,0},{96,32},{1,65},{33,97},{65,1},{97,33},{2,66}... | collective-permute-start | bytes 1867784 | tf_op jit(solution)/shard_map/ppermute | solution.py:435
  50.8 21.2 %collective-permute-start.13 = (bf16[128,1280]{1,0:T(8,128)(2,1)S(1)}, bf16[128,1280]{1,0:T(8,128)(2,1)S(1)}, u32[]{:S(2)}, u32[]{:S(2)}) collective-permute-start(bf16[128,1280]{1,0:T(8,128)(2,1)S(1)} %get-tuple-element.60), channel_id=1, source_target_pairs={{0,96},{32,0},{64,32},{96,64},{1,97},{33,1},{65,33},{97,65},{2,98}... | collective-permute-start | bytes 983048 | tf_op jit(solution)/shard_map/ppermute | solution.py:435
  53.5 18.5 %collective-permute-start.14 = (bf16[128,1280]{1,0:T(8,128)(2,1)S(1)}, bf16[128,1280]{1,0:T(8,128)(2,1)S(1)}, u32[]{:S(2)}, u32[]{:S(2)}) collective-permute-start(bf16[128,1280]{1,0:T(8,128)(2,1)S(1)} %get-tuple-element.61), channel_id=1, source_target_pairs={{0,32},{32,64},{64,96},{96,0},{1,33},{33,65},{65,97},{97,1},{2,34}... | collective-permute-start | bytes 983048 | tf_op jit(solution)/shard_map/ppermute | solution.py:435
  53.5 45.9 %slice-start = ((s8[5242880]{0:T(1024)(128)(4,1)}), s8[4194304]{0:T(1024)(128)(4,1)S(1)}, s32[]{:S(2)}) async-start(s8[5242880]{0:T(1024)(128)(4,1)} %bitcast), calls=%async_computation | async-start | bytes 8388608
  53.5 45.9 %slice-start.2 = ((s8[5242880]{0:T(1024)(128)(4,1)}), s8[4194304]{0:T(1024)(128)(4,1)S(1)}, s32[]{:S(2)}) async-start(s8[5242880]{0:T(1024)(128)(4,1)} %bitcast.2), calls=%async_computation.2 | async-start | bytes 8388608
  53.5 45.9 %slice-start.1 = ((s8[5242880]{0:T(1024)(128)(4,1)}), s8[1048576]{0:T(1024)(128)(4,1)S(1)}, s32[]{:S(2)}) async-start(s8[5242880]{0:T(1024)(128)(4,1)} %bitcast), calls=%async_computation.1 | async-start | bytes 2097152
  53.5 45.9 %slice-start.3 = ((s8[5242880]{0:T(1024)(128)(4,1)}), s8[1048576]{0:T(1024)(128)(4,1)S(1)}, s32[]{:S(2)}) async-start(s8[5242880]{0:T(1024)(128)(4,1)} %bitcast.2), calls=%async_computation.3 | async-start | bytes 2097152
  59.6 8.0 %collective-permute-start.10 = (bf16[384,256]{1,0:T(8,128)(2,1)S(1)}, bf16[384,256]{1,0:T(8,128)(2,1)S(1)}, u32[]{:S(2)}, u32[]{:S(2)}) collective-permute-start(bf16[384,256]{1,0:T(8,128)(2,1)S(1)} %get-tuple-element.57), channel_id=1, source_target_pairs={{0,8},{4,12},{8,16},{12,20},{16,24},{20,28},{24,0},{28,4},{1,9},{5... | collective-permute-start | bytes 589832 | tf_op jit(solution)/shard_map/ppermute | solution.py:435
  60.9 11.1 %collective-permute-start.11 = (bf16[384,256]{1,0:T(8,128)(2,1)S(1)}, bf16[384,256]{1,0:T(8,128)(2,1)S(1)}, u32[]{:S(2)}, u32[]{:S(2)}) collective-permute-start(bf16[384,256]{1,0:T(8,128)(2,1)S(1)} %get-tuple-element.58), channel_id=1, source_target_pairs={{0,16},{4,20},{8,24},{12,28},{16,0},{20,4},{24,8},{28,12},{1,17},{... | collective-permute-start | bytes 589832 | tf_op jit(solution)/shard_map/ppermute | solution.py:435
  63.3 8.7 %collective-permute-start.12 = (bf16[384,256]{1,0:T(8,128)(2,1)S(1)}, bf16[384,256]{1,0:T(8,128)(2,1)S(1)}, u32[]{:S(2)}, u32[]{:S(2)}) collective-permute-start(bf16[384,256]{1,0:T(8,128)(2,1)S(1)} %get-tuple-element.59), channel_id=1, source_target_pairs={{0,24},{4,28},{8,0},{12,4},{16,8},{20,12},{24,16},{28,20},{1,25},{... | collective-permute-start | bytes 589832 | tf_op jit(solution)/shard_map/ppermute | solution.py:435
  72.1 1.3 %collective-permute-start.17 = (bf16[128,256]{1,0:T(8,128)(2,1)S(1)}, bf16[128,256]{1,0:T(8,128)(2,1)S(1)}, u32[]{:S(2)}, u32[]{:S(2)}) collective-permute-start(bf16[128,256]{1,0:T(8,128)(2,1)S(1)} %get-tuple-element.75), channel_id=1, source_target_pairs={{0,1},{1,0},{2,3},{3,2},{4,5},{5,4},{6,7},{7,6},{8,9},{9,8},{10,11... | collective-permute-start | bytes 196616 | tf_op jit(solution)/shard_map/ppermute | solution.py:435
  73.5 7.8 %collective-permute-start.20 = (bf16[128,256]{1,0:T(8,128)(2,1)S(1)}, bf16[128,256]{1,0:T(8,128)(2,1)S(1)}, u32[]{:S(2)}, u32[]{:S(2)}) collective-permute-start(bf16[128,256]{1,0:T(8,128)(2,1)S(1)} %add_convert_fusion.1), channel_id=1, source_target_pairs={{0,6},{1,7},{2,0},{3,1},{4,2},{5,3},{6,4},{7,5},{8,14},{9,15},{10,... | collective-permute-start | bytes 196616 | tf_op jit(solution)/shard_map/ppermute | solution.py:435
  75.4 6.2 %collective-permute-start.19 = (bf16[128,256]{1,0:T(8,128)(2,1)S(1)}, bf16[128,256]{1,0:T(8,128)(2,1)S(1)}, u32[]{:S(2)}, u32[]{:S(2)}) collective-permute-start(bf16[128,256]{1,0:T(8,128)(2,1)S(1)} %add_convert_fusion.1), channel_id=1, source_target_pairs={{0,4},{1,5},{2,6},{3,7},{4,0},{5,1},{6,2},{7,3},{8,12},{9,13},{10,... | collective-permute-start | bytes 196616 | tf_op jit(solution)/shard_map/ppermute | solution.py:435
  76.2 6.7 %collective-permute-start.18 = (bf16[128,256]{1,0:T(8,128)(2,1)S(1)}, bf16[128,256]{1,0:T(8,128)(2,1)S(1)}, u32[]{:S(2)}, u32[]{:S(2)}) collective-permute-start(bf16[128,256]{1,0:T(8,128)(2,1)S(1)} %add_convert_fusion.1), channel_id=1, source_target_pairs={{0,2},{1,3},{2,4},{3,5},{4,6},{5,7},{6,0},{7,1},{8,10},{9,11},{10,... | collective-permute-start | bytes 196616 | tf_op jit(solution)/shard_map/ppermute | solution.py:435
  77.1 11.2 %collective-permute-start.16 = (bf16[128,1280]{1,0:T(8,128)(2,1)S(1)}, bf16[128,1280]{1,0:T(8,128)(2,1)S(1)}, u32[]{:S(2)}, u32[]{:S(2)}) collective-permute-start(bf16[128,1280]{1,0:T(8,128)(2,1)S(1)} %get-tuple-element.69), channel_id=1, source_target_pairs={{0,64},{32,96},{64,0},{96,32},{1,65},{33,97},{65,1},{97,33},{2,66}... | collective-permute-start | bytes 983048 | tf_op jit(solution)/shard_map/ppermute | solution.py:435
  78.3 6.6 %collective-permute-start.15 = (bf16[128,256]{1,0:T(8,128)(2,1)S(1)}, bf16[128,256]{1,0:T(8,128)(2,1)S(1)}, u32[]{:S(2)}, u32[]{:S(2)}) collective-permute-start(bf16[128,256]{1,0:T(8,128)(2,1)S(1)} %get-tuple-element.68), channel_id=1, source_target_pairs={{0,4},{4,0},{8,12},{12,8},{16,20},{20,16},{24,28},{28,24},{1,5},{5... | collective-permute-start | bytes 196616 | tf_op jit(solution)/shard_map/ppermute | solution.py:435
  83.0 12.2 %collective-permute-start.22 = (bf16[128,256]{1,0:T(8,128)(2,1)S(1)}, bf16[128,256]{1,0:T(8,128)(2,1)S(1)}, u32[]{:S(2)}, u32[]{:S(2)}) collective-permute-start(bf16[128,256]{1,0:T(8,128)(2,1)S(1)} %add_convert_fusion), channel_id=1, source_target_pairs={{0,8},{1,25},{2,10},{3,27},{4,12},{5,29},{6,14},{7,31},{8,40},{9,5... | collective-permute-start | bytes 196616 | tf_op jit(solution)/shard_map/ppermute | solution.py:435
  84.2 11.0 %collective-permute-start.21 = (bf16[128,256]{1,0:T(8,128)(2,1)S(1)}, bf16[128,256]{1,0:T(8,128)(2,1)S(1)}, u32[]{:S(2)}, u32[]{:S(2)}) collective-permute-start(bf16[128,256]{1,0:T(8,128)(2,1)S(1)} %add_convert_fusion), channel_id=1, source_target_pairs={{0,0},{1,17},{2,2},{3,19},{4,4},{5,21},{6,6},{7,23},{8,32},{9,49},... | collective-permute-start | bytes 196616 | tf_op jit(solution)/shard_map/ppermute | solution.py:435
  88.4 8.4 %collective-permute-start.27 = (bf16[128,256]{1,0:T(8,128)(2,1)S(1)}, bf16[128,256]{1,0:T(8,128)(2,1)S(1)}, u32[]{:S(2)}, u32[]{:S(2)}) collective-permute-start(bf16[128,256]{1,0:T(8,128)(2,1)S(1)} %add_convert_fusion.2.p0), channel_id=1, source_target_pairs={{0,32},{32,64},{64,96},{96,0},{1,33},{33,65},{65,97},{97,1},{2,34}... | collective-permute-start | bytes 196616 | tf_op jit(solution)/shard_map/ppermute | solution.py:435
  88.4 9.7 %collective-permute-start.26 = (bf16[128,256]{1,0:T(8,128)(2,1)S(1)}, bf16[128,256]{1,0:T(8,128)(2,1)S(1)}, u32[]{:S(2)}, u32[]{:S(2)}) collective-permute-start(bf16[128,256]{1,0:T(8,128)(2,1)S(1)} %add_convert_fusion.2.p0), channel_id=1, source_target_pairs={{0,64},{32,96},{64,0},{96,32},{1,65},{33,97},{65,1},{97,33},{2,66}... | collective-permute-start | bytes 196616 | tf_op jit(solution)/shard_map/ppermute | solution.py:435
  95.1 4.3 %collective-permute-start.25 = (bf16[128,256]{1,0:T(8,128)(2,1)S(1)}, bf16[128,256]{1,0:T(8,128)(2,1)S(1)}, u32[]{:S(2)}, u32[]{:S(2)}) collective-permute-start(bf16[128,256]{1,0:T(8,128)(2,1)S(1)} %add_convert_fusion.2.p0), channel_id=1, source_target_pairs={{0,96},{32,0},{64,32},{96,64},{1,97},{33,1},{65,33},{97,65},{2,98}... | collective-permute-start | bytes 196616 | tf_op jit(solution)/shard_map/ppermute | solution.py:435
  95.1 4.3 %collective-permute-start.24 = (bf16[128,256]{1,0:T(8,128)(2,1)S(1)}, bf16[128,256]{1,0:T(8,128)(2,1)S(1)}, u32[]{:S(2)}, u32[]{:S(2)}) collective-permute-start(bf16[128,256]{1,0:T(8,128)(2,1)S(1)} %collective-permute-done.22.d1), channel_id=1, source_target_pairs={{0,1},{1,0},{2,3},{3,2},{4,5},{5,4},{6,7},{7,6},{8,9},{9,8},{10,11... | collective-permute-start | bytes 196616 | tf_op jit(solution)/shard_map/ppermute | solution.py:435
  95.2 4.2 %collective-permute-start.23 = (bf16[128,256]{1,0:T(8,128)(2,1)S(1)}, bf16[128,256]{1,0:T(8,128)(2,1)S(1)}, u32[]{:S(2)}, u32[]{:S(2)}) collective-permute-start(bf16[128,256]{1,0:T(8,128)(2,1)S(1)} %collective-permute-done.21.d0), channel_id=1, source_target_pairs={{0,1},{1,0},{2,3},{3,2},{4,5},{5,4},{6,7},{7,6},{8,9},{9,8},{10,11... | collective-permute-start | bytes 196616 | tf_op jit(solution)/shard_map/ppermute | solution.py:435
  (5 other events, 121.6 us)
